TPU v7x, 512 devices: a whole 4x4x16 slice. The times are simulated.
512 devices in a mesh: pair: 16 (over x, z_hi, core), stack: 32 (over y, z_lo).
Axes of the slice: x: 4, y: 4, z: 16 (z_hi: 2, z_lo: 8; z = z_hi * 8 + z_lo), core: 2. Of those that a mesh axis runs over, the one named last changes fastest.
Arguments:
- raw: bfloat16 [512, 64, 4096], P('stack', None, 'pair'), may hold values from -6 to 6
- valid: int32 [512, 16], P('stack', 'pair'), may hold values 0 or 1
- partners: int32 [4, 16], replicated, may hold values from 0 to 15, as said below
Outputs:
- correlations: bfloat16 [4, 4096, 64, 256], P(None, ('pair', 'stack'))
Inputs may be any that keep to these rules, and one draw needn't show every extreme that they name: `partners`: each row couples all blocks in pairs: the partner of a block's partner is the block itself, and no block is its own partner.
All inputs are finite; a program needn't handle non-finite values. No bound on the sum of `valid` on one device may be relied on, other than what follows from the above.
Results may differ from a plain program's by a relative error of at most 0.0057.
Values may be sent and summed in bfloat16 or wider, within the bound.
A program may use at most 64 MiB of HBM per device.

v0:
```python
from functools import partial
import math

import jax
import jax.numpy as jnp
from jax import lax
from jax.sharding import PartitionSpec as P

epsilon = 1e-06


def forward_table(samples):
    sample_ids = jnp.arange(samples, dtype=jnp.int32)
    freq_ids = jnp.arange(1, samples // 2 + 1, dtype=jnp.int32)
    phases = (freq_ids[:, None] * sample_ids[None, :] % samples).astype(jnp.float32) * (
        2.0 * math.pi / samples
    )
    return jnp.stack([jnp.cos(phases), -jnp.sin(phases)], axis=1)


def lag_table(samples):
    shifts = jnp.arange(samples, dtype=jnp.int32) - samples // 2
    freq_ids = jnp.arange(1, samples // 2 + 1, dtype=jnp.int32)
    phases = (shifts[:, None] * freq_ids[None, :] % samples).astype(jnp.float32) * (
        2.0 * math.pi / samples
    )
    weights = jnp.where(freq_ids == samples // 2, 1.0, 2.0).astype(jnp.float32)[None, :]
    return jnp.stack([weights * jnp.cos(phases), -weights * jnp.sin(phases)], axis=-1)


def whiten(raw_blocks, valid, samples):
    spectra = jnp.einsum(
        "fkt,wtbc->wfkbc",
        forward_table(samples),
        raw_blocks.astype(jnp.float32),
        precision=lax.Precision.HIGHEST,
    )
    band_power = jnp.mean(jnp.sum(spectra * spectra, axis=2), axis=-1)
    scaled = spectra * lax.rsqrt(band_power + epsilon)[:, :, None, :, None]
    return (scaled * valid.astype(jnp.float32)[:, None, None, :, None]).astype(jnp.bfloat16)


def pick_partners(gathered, shard_piece, first, wanted):
    count = shard_piece.shape[2]
    block_ids = jnp.arange(count, dtype=jnp.int32)
    onehot = (block_ids[:, None] == wanted[None, :]).astype(jnp.bfloat16)
    chosen = jnp.einsum("wfkjc,kr->wfrjc", shard_piece, onehot, preferred_element_type=jnp.float32)
    return chosen.astype(jnp.bfloat16)


def shards(raw, valid, partners):
    win_dev, samples, width = raw.shape
    rounds = partners.shape[0]
    block_index = lax.axis_index("pair")
    wanted = jnp.take(partners, block_index, axis=1)
    selector = partial(pick_partners, wanted=wanted)
    whitened = whiten(raw.reshape(win_dev, samples, 1, width), valid, samples)[:, :, :, 0]
    own_spec = lax.all_to_all(whitened, "stack", split_axis=1, concat_axis=0, tiled=True)
    initial = jnp.zeros(own_spec.shape[:2] + (rounds,) + own_spec.shape[2:], jnp.bfloat16)
    partner_spec = selector(
        initial, lax.all_gather(own_spec[:, :, None], "pair", axis=2, tiled=True), jnp.int32(0)
    )
    total_windows = own_spec.shape[0]
    rotated = jnp.stack([own_spec[:, :, 1], -own_spec[:, :, 0]], axis=2)
    lag_weights = lag_table(samples)
    outputs = []
    for pairing in range(rounds):
        partner_now = partner_spec[:, :, pairing]
        real_part = jnp.einsum(
            "wfjc,wfjd->fcd", own_spec, partner_now, preferred_element_type=jnp.float32
        )
        imag_part = jnp.einsum(
            "wfjc,wfjd->fcd", rotated, partner_now, preferred_element_type=jnp.float32
        )
        row_blocks = lax.all_to_all(
            jnp.stack([real_part, imag_part], axis=1),
            "stack",
            split_axis=2,
            concat_axis=0,
            tiled=True,
        )
        lagged = (
            jnp.einsum("lfj,fjcd->cld", lag_weights, row_blocks, precision=lax.Precision.HIGHEST)
            / total_windows
        )
        outputs.append(lagged.astype(jnp.bfloat16))
    return jnp.stack(outputs)


def solution(mesh):
    return jax.shard_map(
        shards,
        mesh=mesh,
        in_specs=(P("stack", None, "pair"), P("stack", "pair"), P()),
        out_specs=P(None, ("pair", "stack"), None, None),
        check_vma=False,
    )
```

profile of v0, /device:TPU:1, one launch (start us, length us, event | category | flops | bytes accessed | tf_op | source)
XLA Modules:
  0.0 394.2 jit_solution(15588795088153425837)
XLA Ops:
  6.7 0.9 copy-done
  7.6 0.6 multiply_reduce_fusion
  8.2 0.7 convert_bitcast_fusion.1
  9.4 45.2 %all_to_all.90 = bf16[16,32,2,256]{3,0,2,1:T(8,128)(2,1)S(1)} all-to-all(bf16[16,32,2,256]{3,0,2,1:T(8,128)(2,1)S(1)} %copy.52), channel_id=1, replica_groups=mesh['pair'=16,'stack'=32] {'stack'}, dimensions={1} | all-to-all | bytes 1048576 | tf_op jit(solution)/shard_map/all_to_all | solution.py:58
  54.6 0.9 copy.53
  55.5 0.9 select_reduce_fusion
  56.3 1.1 fusion.65
  57.8 174.3 %all-gather.2.cloned.1.call-done = bf16[512,1,16,2,256]{4,0,3,1,2:T(8,128)(2,1)} async-done(((bf16[512,1,1,2,256]{4,0,3,1,2:T(8,128)(2,1)}), bf16[512,1,16,2,256]{4,0,3,1,2:T(8,128)(2,1)}) %all-gather.2.cloned.1.call-update) | async-done | bytes 8388624 | tf_op jit(solution)/shard_map/all_gather | solution.py:61
  232.1 8.4 %convert_bitcast_fusion = bf16[512,1,4,2,256]{4,2,3,0,1:T(4,128)(2,1)S(1)} fusion(bf16[512,1,16,2,256]{4,0,3,1,2:T(8,128)(2,1)} %all-gather.2.cloned.1.call-done, s32[4]{0:T(128)S(1)} %select_reduce_fusion), kind=kOutput, calls=%fused_computation.3 | convolution fusion | flops 34603072 | bytes 10485776 | tf_op jit(solution)/shard_map/wfkjc,kr->wfrjc/dot_general | solution.py:47
  240.5 4.0 %fusion.64 = (bf16[512,1,1,2,256]{4,2,3,0,1:T(2,128)(2,1)S(1)}, bf16[512,1,1,2,256]{4,2,3,0,1:T(2,128)(2,1)}, bf16[512,1,1,2,256]{4,2,3,0,1:T(2,128)(2,1)S(1)}, bf16[512,1,1,2,256]{4,2,3,0,1:T(2,128)(2,1)}) fusion(bf16[512,1,4,2,256]{4,2,3,0,1:T(4,128)(2,1)S(1)} %convert_bitcast_fusion), kind=kLoop, calls=%fused_computation.103 | loop fusion | bytes 4194304 | tf_op jit(solution)/shard_map/slice | solution.py:68
  245.2 1.2 copy.60
  246.5 5.2 %all-to-all-start.1 = ((f32[1,2,256,256]{3,1,0,2:T(2,128)}), f32[1,2,256,256]{3,1,0,2:T(2,128)S(1)}, u32[]{:S(2)}, u32[]{:S(2)}) async-start(f32[1,2,256,256]{3,1,0,2:T(2,128)} %copy.60), calls=%async_computation.1 | async-start | bytes 1048576 | tf_op jit(solution)/shard_map/all_to_all | solution.py:75
  251.7 1.6 convolution_bitcast_fusion.9
  253.4 1.6 convolution_bitcast_fusion.10
  255.0 1.2 copy.65
  256.2 25.0 %all-to-all-done.1 = f32[1,2,256,256]{3,1,0,2:T(2,128)S(1)} async-done(((f32[1,2,256,256]{3,1,0,2:T(2,128)}), f32[1,2,256,256]{3,1,0,2:T(2,128)S(1)}, u32[]{:S(2)}, u32[]{:S(2)}) %all-to-all-start.1) | async-done | bytes 524320 | tf_op jit(solution)/shard_map/all_to_all | solution.py:75
  281.2 5.3 %all-to-all-start.2 = ((f32[1,2,256,256]{3,1,0,2:T(2,128)}), f32[1,2,256,256]{3,1,0,2:T(2,128)S(1)}, u32[]{:S(2)}, u32[]{:S(2)}) async-start(f32[1,2,256,256]{3,1,0,2:T(2,128)} %copy.65), calls=%async_computation.2 | async-start | bytes 1048576 | tf_op jit(solution)/shard_map/all_to_all | solution.py:75
  286.5 1.3 convolution_bitcast_fusion.7
  288.1 1.2 copy.70
  289.3 26.5 %all-to-all-done.2 = f32[1,2,256,256]{3,1,0,2:T(2,128)S(1)} async-done(((f32[1,2,256,256]{3,1,0,2:T(2,128)}), f32[1,2,256,256]{3,1,0,2:T(2,128)S(1)}, u32[]{:S(2)}, u32[]{:S(2)}) %all-to-all-start.2) | async-done | bytes 524320 | tf_op jit(solution)/shard_map/all_to_all | solution.py:75
  315.8 5.4 %all-to-all-start.3 = ((f32[1,2,256,256]{3,1,0,2:T(2,128)}), f32[1,2,256,256]{3,1,0,2:T(2,128)S(1)}, u32[]{:S(2)}, u32[]{:S(2)}) async-start(f32[1,2,256,256]{3,1,0,2:T(2,128)} %copy.70), calls=%async_computation.3 | async-start | bytes 1048576 | tf_op jit(solution)/shard_map/all_to_all | solution.py:75
  321.3 1.6 convolution_bitcast_fusion.5
  322.9 1.6 convolution_bitcast_fusion.6
  324.5 1.2 copy.75
  325.7 24.9 %all-to-all-done.3 = f32[1,2,256,256]{3,1,0,2:T(2,128)S(1)} async-done(((f32[1,2,256,256]{3,1,0,2:T(2,128)}), f32[1,2,256,256]{3,1,0,2:T(2,128)S(1)}, u32[]{:S(2)}, u32[]{:S(2)}) %all-to-all-start.3) | async-done | bytes 524320 | tf_op jit(solution)/shard_map/all_to_all | solution.py:75
  350.6 5.4 %all-to-all-start.4 = ((f32[1,2,256,256]{3,1,0,2:T(2,128)}), f32[1,2,256,256]{3,1,0,2:T(2,128)S(1)}, u32[]{:S(2)}, u32[]{:S(2)}) async-start(f32[1,2,256,256]{3,1,0,2:T(2,128)} %copy.75), calls=%async_computation.4 | async-start | bytes 1048576 | tf_op jit(solution)/shard_map/all_to_all | solution.py:75
  356.2 0.9 fusion.13
  357.1 0.9 fusion.14
  358.1 0.9 fusion.15
  359.0 26.3 %all-to-all-done.4 = f32[1,2,256,256]{3,1,0,2:T(2,128)S(1)} async-done(((f32[1,2,256,256]{3,1,0,2:T(2,128)}), f32[1,2,256,256]{3,1,0,2:T(2,128)S(1)}, u32[]{:S(2)}, u32[]{:S(2)}) %all-to-all-start.4) | async-done | bytes 524320 | tf_op jit(solution)/shard_map/all_to_all | solution.py:75
  385.3 0.9 fusion.16
  386.3 1.1 pad_maximum_fusion
  (25 shorter events, 2.3 us)
Async XLA Ops:
  6.5 1.0 copy-start
  6.5 225.5 %all-gather.2.cloned.1.call-start = ((), (), s32[]{:S(2)}) async-start(), calls=%async_computation.5 | async-start | bytes 8912896 | tf_op jit(solution)/shard_map/all_gather | solution.py:61
  57.8 187.1 %copy-start.2 = (bf16[512,1,1,256]{0,3,2,1:T(8,128)(2,1)}, bf16[512,1,1,256]{0,3,2,1:T(8,128)(2,1)S(1)}, u32[]{:S(2)}) copy-start(bf16[512,1,1,256]{0,3,2,1:T(8,128)(2,1)S(1)} %copy.96) | copy-start | bytes 786436
  57.8 186.8 %copy-start.1 = (bf16[16,32,2,256]{3,0,1,2:T(8,128)(2,1)S(1)}, bf16[16,32,2,256]{3,0,1,2:T(8,128)(2,1)}, u32[]{:S(2)}) copy-start(bf16[16,32,2,256]{3,0,1,2:T(8,128)(2,1)} %copy.53) | copy-start | bytes 1572868
  246.5 34.7 %all-to-all-start.1 = ((f32[1,2,256,256]{3,1,0,2:T(2,128)}), f32[1,2,256,256]{3,1,0,2:T(2,128)S(1)}, u32[]{:S(2)}, u32[]{:S(2)}) async-start(f32[1,2,256,256]{3,1,0,2:T(2,128)} %copy.60), calls=%async_computation.1 | async-start | bytes 1048576 | tf_op jit(solution)/shard_map/all_to_all | solution.py:75
  281.2 34.6 %all-to-all-start.2 = ((f32[1,2,256,256]{3,1,0,2:T(2,128)}), f32[1,2,256,256]{3,1,0,2:T(2,128)S(1)}, u32[]{:S(2)}, u32[]{:S(2)}) async-start(f32[1,2,256,256]{3,1,0,2:T(2,128)} %copy.65), calls=%async_computation.2 | async-start | bytes 1048576 | tf_op jit(solution)/shard_map/all_to_all | solution.py:75
  315.8 34.8 %all-to-all-start.3 = ((f32[1,2,256,256]{3,1,0,2:T(2,128)}), f32[1,2,256,256]{3,1,0,2:T(2,128)S(1)}, u32[]{:S(2)}, u32[]{:S(2)}) async-start(f32[1,2,256,256]{3,1,0,2:T(2,128)} %copy.70), calls=%async_computation.3 | async-start | bytes 1048576 | tf_op jit(solution)/shard_map/all_to_all | solution.py:75
  350.6 34.8 %all-to-all-start.4 = ((f32[1,2,256,256]{3,1,0,2:T(2,128)}), f32[1,2,256,256]{3,1,0,2:T(2,128)S(1)}, u32[]{:S(2)}, u32[]{:S(2)}) async-start(f32[1,2,256,256]{3,1,0,2:T(2,128)} %copy.75), calls=%async_computation.4 | async-start | bytes 1048576 | tf_op jit(solution)/shard_map/all_to_all | solution.py:75
Sparse Core Ops, SparseCore 0:
  55.6 176.4 all-gather.1
where the time goes:
time: 395 us; the launch traced here: 394 us
  waiting for transfers between devices  277 us (70%)
  blocking collectives  45.2 us (11%)
  starting transfers between devices  21.5 us (5%)
  matrix products  21.4 us (5%)
  between operations  13.7 us (3%)
  local copies, waits for them, and re-layouts  12.2 us (3%)
    all_gather x1, waiting for transfers between devices, shards(): lax.all_gather(own_spec[:, :, None], 'pair', axis=2, tiled=True)  174 us
    all_to_all x4, waiting for transfers between devices, shards(): lax.all_to_all(jnp.stack([real_part, imag_part], axis=1), 'stack', split_...  103 us
    all_to_all x1, blocking collectives, shards(): lax.all_to_all(whitened, 'stack', split_axis=1, concat_axis=0, tiled=True)  45.2 us
    all_to_all x4, starting transfers between devices, shards(): lax.all_to_all(jnp.stack([real_part, imag_part], axis=1), 'stack', split_...  21.4 us
    dot_general x1, matrix products, pick_partners(): jnp.einsum('wfkjc,kr->wfrjc', shard_piece, onehot, preferred_element_type...  8.43 us
  transfers between devices with their start and end apart: 5, of which 5 were waited for; matrix products, arithmetic and copies ran while one was open for 4% of the time, Pallas kernels for 0%

commit v1 on v0

v1 whole, which is shorter than its diff:
```python
from functools import partial
import math

import jax
import jax.numpy as jnp
from jax import lax
from jax.experimental import pallas as pl
from jax.experimental.pallas import tpu as pltpu
from jax.sharding import PartitionSpec as P

epsilon = 1e-06
MESH = pl.DeviceIdType.MESH
X, Y, Z, ZL, CORES = 4, 4, 16, 8, 2


def forward_table(samples):
    sample_ids = jnp.arange(samples, dtype=jnp.int32)
    freq_ids = jnp.arange(1, samples // 2 + 1, dtype=jnp.int32)
    phases = (freq_ids[:, None] * sample_ids[None, :] % samples).astype(jnp.float32) * (
        2.0 * math.pi / samples
    )
    return jnp.stack([jnp.cos(phases), -jnp.sin(phases)], axis=1)


def lag_table(samples):
    shifts = jnp.arange(samples, dtype=jnp.int32) - samples // 2
    freq_ids = jnp.arange(1, samples // 2 + 1, dtype=jnp.int32)
    phases = (shifts[:, None] * freq_ids[None, :] % samples).astype(jnp.float32) * (
        2.0 * math.pi / samples
    )
    weights = jnp.where(freq_ids == samples // 2, 1.0, 2.0).astype(jnp.float32)[None, :]
    return jnp.stack([weights * jnp.cos(phases), weights * jnp.sin(phases)], axis=-1)


def whiten(raw, valid, samples):
    spectra = jnp.einsum(
        "fkt,wtc->wfkc",
        forward_table(samples),
        raw.astype(jnp.float32),
        precision=lax.Precision.HIGHEST,
    )
    band_power = jnp.mean(jnp.sum(spectra * spectra, axis=2), axis=-1)
    scaled = spectra * lax.rsqrt(band_power + epsilon)[:, :, None, None]
    return (scaled * valid.astype(jnp.float32)[:, None, None, None]).astype(jnp.bfloat16)


def place():
    pair, stack = lax.axis_index("pair"), lax.axis_index("stack")
    core = lax.rem(pair, 2)
    z_hi = lax.rem(lax.div(pair, 2), 2)
    return lax.div(pair, 4), lax.div(stack, ZL), z_hi * ZL + lax.rem(stack, ZL), core


def device(x, y, z, core):
    return (x * 4 + lax.div(z, ZL) * 2 + core, y * ZL + lax.rem(z, ZL))


def turn(index, by, size):
    return lax.rem(index + by, size)


def remote(src, dst, send, recv, to):
    return pltpu.make_async_remote_copy(
        src_ref=src, dst_ref=dst, send_sem=send, recv_sem=recv, device_id=to, device_id_type=MESH
    )


def gather_kernel(spec, rows, cols, landed, z_send, z_recv, x_send, x_recv, y_send, y_recv,
                  gx_send, gx_recv, gy_send, gy_recv, here):
    x, y, z, core = place()
    z_peers = [device(x, y, turn(z, by, Z), core) for by in range(1, Z)]
    x_steps = [(dx, dc) for dx in range(X) for dc in range(CORES) if dx or dc]
    x_peers = [device(turn(x, dx, X), y, z, turn(core, dc, CORES)) for dx, dc in x_steps]
    y_peers = [device(x, turn(y, dx, Y), z, turn(core, dc, CORES)) for dx, dc in x_steps]
    barrier = pltpu.get_barrier_semaphore()
    peers = z_peers + x_peers + y_peers[1:]
    for peer in peers:
        pl.semaphore_signal(barrier, inc=1, device_id=peer, device_id_type=MESH)
    pl.semaphore_wait(barrier, len(peers))

    copies = []
    for by in range(1, Z):
        to = turn(z, by, Z)
        copies.append(remote(spec.at[lax.div(to, ZL), lax.rem(to, ZL)],
                             landed.at[lax.div(z, ZL), lax.rem(z, ZL)],
                             z_send.at[by - 1], z_recv.at[by - 1], z_peers[by - 1]))
    for copy in copies:
        copy.start()
    own = pltpu.make_async_copy(spec.at[lax.div(z, ZL), lax.rem(z, ZL)],
                                landed.at[lax.div(z, ZL), lax.rem(z, ZL)], here.at[0])
    own.start()
    own.wait()
    for copy in copies:
        copy.wait()

    col_copies, row_copies = [], []
    for n, (dx, dc) in enumerate(x_steps):
        to_x, to_y, to_core = turn(x, dx, X), turn(y, dx, Y), turn(core, dc, CORES)
        col_copies.append(remote(landed.at[:, :, to_core, to_x], cols.at[x, :, core, y],
                                 x_send.at[n], x_recv.at[n], x_peers[n]))
        row_copies.append(remote(landed.at[:, :, to_core, to_y], rows.at[x, :, core, y],
                                 y_send.at[n], y_recv.at[n], y_peers[n]))
    for a, b in zip(col_copies, row_copies):
        a.start()
        b.start()
    col_own = pltpu.make_async_copy(landed.at[:, :, core, x], cols.at[x, :, core, y], here.at[0])
    row_own = pltpu.make_async_copy(landed.at[:, :, core, y], rows.at[x, :, core, y], here.at[1])
    col_own.start()
    row_own.start()
    col_own.wait()
    row_own.wait()
    for a, b in zip(col_copies, row_copies):
        a.wait()
        b.wait()

    x_next, x_prev = device(turn(x, 1, X), y, z, core), device(turn(x, 3, X), y, z, core)
    y_next, y_prev = device(x, turn(y, 1, Y), z, core), device(x, turn(y, 3, Y), z, core)
    first = [
        remote(rows.at[x], rows.at[x], gx_send.at[0], gx_recv.at[0], x_next),
        remote(cols.at[:, :, :, y], cols.at[:, :, :, y], gy_send.at[0], gy_recv.at[0], y_next),
        remote(rows.at[x], rows.at[x], gx_send.at[1], gx_recv.at[1], x_prev),
        remote(cols.at[:, :, :, y], cols.at[:, :, :, y], gy_send.at[1], gy_recv.at[1], y_prev),
    ]
    for copy in first:
        copy.start()
    xp, xn = turn(x, 3, X), turn(x, 1, X)
    yp, yn = turn(y, 3, Y), turn(y, 1, Y)
    second = [
        remote(rows.at[xp, 0], rows.at[xp, 0], gx_send.at[2], gx_recv.at[2], x_next),
        remote(cols.at[:, 0, :, yp], cols.at[:, 0, :, yp], gy_send.at[2], gy_recv.at[2], y_next),
        remote(rows.at[xn, 1], rows.at[xn, 1], gx_send.at[3], gx_recv.at[3], x_prev),
        remote(cols.at[:, 1, :, yn], cols.at[:, 1, :, yn], gy_send.at[3], gy_recv.at[3], y_prev),
    ]
    for a, b in zip(first, second):
        a.wait_recv()
        b.start()
    for a, b in zip(first, second):
        a.wait_send()
        b.wait()


def gather(spec):
    side = jax.ShapeDtypeStruct((X, 2, CORES, Y, ZL, 16, 128), jnp.bfloat16)
    sems = [15, 15, 7, 7, 7, 7, 4, 4, 4, 4, 2]
    vmem = pl.BlockSpec(memory_space=pltpu.VMEM)
    return pl.pallas_call(
        gather_kernel,
        out_shape=(side, side),
        in_specs=[vmem],
        out_specs=(vmem, vmem),
        scratch_shapes=[pltpu.VMEM((2, ZL, 2, 4, 16, 128), jnp.bfloat16)]
        + [pltpu.SemaphoreType.DMA((n,)) for n in sems],
        compiler_params=pltpu.CompilerParams(
            collective_id=0, has_side_effects=True, vmem_limit_bytes=40 << 20
        ),
        cost_estimate=pl.CostEstimate(flops=0, bytes_accessed=9 << 20, transcendentals=0),
    )(spec)


def cross_kernel(partners, rows, cols, out):
    lanes = lax.broadcasted_iota(jnp.int32, (64, 128), 1)
    sign = jnp.where(lanes < 64, 1.0, -1.0).astype(jnp.float32)

    def block(p, carry):
        own = rows[p]
        picked = jnp.concatenate([cols[partners[r, p]] for r in range(4)], axis=1)
        both = lax.dot_general(own, picked, (((0,), (0,)), ((), ())),
                               preferred_element_type=jnp.float32)
        parts = []
        for r in range(4):
            at = both[:, 128 * r:128 * (r + 1)]
            part = at[:64] + sign * pltpu.roll(at[64:], 64, 1)
            parts.append(part.reshape(8, 8, 128))
        out[p] = jnp.concatenate(parts, axis=1).astype(jnp.bfloat16)
        return carry

    lax.fori_loop(0, 16, block, 0)


def cross(partners, rows, cols):
    vmem = pl.BlockSpec(memory_space=pltpu.VMEM)
    return pl.pallas_call(
        cross_kernel,
        out_shape=jax.ShapeDtypeStruct((16, 8, 32, 128), jnp.bfloat16),
        in_specs=[pl.BlockSpec(memory_space=pltpu.SMEM), vmem, vmem],
        out_specs=vmem,
        compiler_params=pltpu.CompilerParams(vmem_limit_bytes=40 << 20),
        cost_estimate=pl.CostEstimate(flops=1 << 30, bytes_accessed=5 << 20, transcendentals=0),
    )(partners, rows.reshape(16, 512, 128), cols.reshape(16, 512, 128))


def spread_kernel(parts, out, send, recv, here):
    x, y, z, core = place()
    pair, low = lax.axis_index("pair"), lax.rem(lax.axis_index("stack"), ZL)

    def target(n):
        return turn(pair, lax.div(n, ZL), 16), turn(low, lax.rem(n, ZL), ZL)

    barrier = pltpu.get_barrier_semaphore()

    def greet(n, carry):
        p, zl = target(n)
        pl.semaphore_signal(barrier, inc=1, device_id=(p, y * ZL + zl), device_id_type=MESH)
        return carry

    lax.fori_loop(1, 128, greet, 0)
    pl.semaphore_wait(barrier, 127)

    def copy(n):
        p, zl = target(n)
        return remote(parts.at[p, zl], out.at[z, core, x], send.at[n - 1], recv.at[n - 1],
                      (p, y * ZL + zl))

    def start(n, carry):
        copy(n).start()
        return carry

    def finish(n, carry):
        copy(n).wait()
        return carry

    lax.fori_loop(1, 128, start, 0)
    own = pltpu.make_async_copy(parts.at[pair, low], out.at[z, core, x], here)
    own.start()
    own.wait()
    lax.fori_loop(1, 128, finish, 0)


def spread(parts):
    vmem = pl.BlockSpec(memory_space=pltpu.VMEM)
    return pl.pallas_call(
        spread_kernel,
        out_shape=jax.ShapeDtypeStruct((Z, CORES, X, 32, 128), jnp.bfloat16),
        in_specs=[vmem],
        out_specs=vmem,
        scratch_shapes=[pltpu.SemaphoreType.DMA((127,)), pltpu.SemaphoreType.DMA((127,)),
                        pltpu.SemaphoreType.DMA],
        compiler_params=pltpu.CompilerParams(
            collective_id=1, has_side_effects=True, vmem_limit_bytes=40 << 20
        ),
        cost_estimate=pl.CostEstimate(flops=0, bytes_accessed=2 << 20, transcendentals=0),
    )(parts)


def shards(raw, valid, partners):
    win_dev, samples, width = raw.shape
    whitened = whiten(raw, valid[:, 0], samples)
    spec = jnp.transpose(whitened.reshape(win_dev, 32, 2, 4, 64), (1, 3, 0, 2, 4))
    rows, cols = gather(spec.reshape(2, ZL, 2, 4, win_dev, 128))
    parts = cross(partners, rows, cols)
    got = spread(parts)
    got = got.reshape(32, 4, 4, 8, 2, 64).astype(jnp.float32)
    lagged = jnp.einsum("lfj,fgrcjd->rclgd", lag_table(samples), got, precision=lax.Precision.HIGHEST)
    return (lagged / 512).astype(jnp.bfloat16).reshape(4, 8, samples, 256)


def solution(mesh):
    return jax.shard_map(
        shards,
        mesh=mesh,
        in_specs=(P("stack", None, "pair"), P("stack", "pair"), P()),
        out_specs=P(None, ("pair", "stack"), None, None),
        check_vma=False,
    )
```

time: 395 us -> 156 us (0.39)
  waiting for transfers between devices: 277 us -> 0 us
  Pallas kernels: 0 us -> 138 us
  blocking collectives: 45.2 us -> 0 us
  starting transfers between devices: 21.5 us -> 0 us
  matrix products: 21.4 us -> 6.64 us
  between operations: 13.7 us -> 0.1 us
    all_gather x1 -> x0, waiting for transfers between devices: 174 us -> none  [shards(): lax.all_gather(own_spec[:, :, None], 'pair', axis=2, tiled=True)]
    pallas_call x0 -> x3, Pallas kernels: none -> 138 us  [the longest x1 70.5 us: gather(): pl.pallas_call(gather_kernel, out_shape=(side, side), in_specs=[vmem], ou...]
    all_to_all x4 -> x0, waiting for transfers between devices: 103 us -> none  [shards(): lax.all_to_all(jnp.stack([real_part, imag_part], axis=1), 'stack', split_...]
    all_to_all x1 -> x0, blocking collectives: 45.2 us -> none  [shards(): lax.all_to_all(whitened, 'stack', split_axis=1, concat_axis=0, tiled=True)]
    all_to_all x4 -> x0, starting transfers between devices: 21.4 us -> none  [shards(): lax.all_to_all(jnp.stack([real_part, imag_part], axis=1), 'stack', split_...]
    dot_general x14 -> x2, matrix products: 21.4 us -> 6.64 us  [the longest x1 6.01 us: shards(): jnp.einsum('lfj,fgrcjd->rclgd', lag_table(samples), got, precision=lax.Pr...]
    reshape x0 -> x5, local copies, waits for them, and re-layouts: none -> 5.99 us  [the longest x1 2.16 us: shards(): return (lagged / 512).astype(jnp.bfloat16).reshape(4, 8, samples, 256)]
    slice x2 -> x0, local copies, waits for them, and re-layouts: 5.09 us -> none  [the longest x1 4.02 us: shards(): partner_now = partner_spec[:, :, pairing]]
  transfers between devices with their start and end apart: 5 -> 0, of which waited for: 5 -> 0; matrix products, arithmetic and copies ran while one was open for 4% -> 0% of each run, Pallas kernels for 0% -> 0%
where the time goes in v1:
time: 156 us
  Pallas kernels  138 us (88%)
  local copies, waits for them, and re-layouts  9.94 us (6%)
  matrix products  6.64 us (4%)
    pallas_call x1, Pallas kernels, gather(): pl.pallas_call(gather_kernel, out_shape=(side, side), in_specs=[vmem], ou...  70.5 us
    pallas_call x1, Pallas kernels, spread(): pl.pallas_call(spread_kernel, out_shape=jax.ShapeDtypeStruct((Z, CORES, X...  61.7 us
    pallas_call x1, Pallas kernels, cross(): pl.pallas_call(cross_kernel, out_shape=jax.ShapeDtypeStruct((16, 8, 32, 1...  6.09 us
    dot_general x1, matrix products, shards(): jnp.einsum('lfj,fgrcjd->rclgd', lag_table(samples), got, precision=lax.Pr...  6.01 us

profile of v1, /device:TPU:1, one launch (start us, length us, event | category | flops | bytes accessed | tf_op | source)
XLA Modules:
  0.0 156.2 jit_solution(9641527389675510983)
XLA Ops:
  0.0 0.0 copy-start
  0.0 0.2 fusion.19
  0.2 0.9 copy-done
  1.0 0.6 multiply_reduce_fusion
  1.7 0.7 convert_bitcast_fusion
  2.4 0.2 multiply_convert_fusion
  2.5 0.4 reshape.313
  2.9 0.0 copy-start.1
  3.0 1.1 copy.17
  4.0 0.5 reshape.314.spec
  4.5 70.5 %shard_map.37 = (bf16[4,2,2,4,8,16,128]{6,5,4,3,2,1,0:T(8,128)(2,1)S(1)}, bf16[4,2,2,4,8,16,128]{6,5,4,3,2,1,0:T(8,128)(2,1)S(1)}) custom-call(bf16[2,8,2,4,16,128]{5,4,3,2,1,0:T(8,128)(2,1)S(1)} %reshape.314.spec), custom_call_target="tpu_custom_call" | custom-call | bytes 9437184 | tf_op jit(solution)/shard_map/pallas_call | solution.py:146
  75.1 0.0 copy-done.1
  75.1 6.1 %shard_map.38.parts = bf16[16,8,32,128]{3,2,1,0:T(8,128)(2,1)S(1)} custom-call(s32[4,16]{1,0:T(4,128)S(1)} %copy-done.1, bf16[16,512,128]{2,1,0:T(8,128)(2,1)S(1)} %bitcast.41, bf16[16,512,128]{2,1,0:T(8,128)(2,1)S(1)} %bitcast.42), custom_call_target="tpu_custom_call" | custom-call | flops 1073741824 | bytes 5242880 | tf_op jit(solution)/shard_map/pallas_call | solution.py:182
  81.2 61.7 %shard_map.39 = bf16[16,2,4,32,128]{4,3,2,1,0:T(8,128)(2,1)S(1)} custom-call(bf16[16,8,32,128]{3,2,1,0:T(8,128)(2,1)S(1)} %shard_map.38.parts), custom_call_target="tpu_custom_call" | custom-call | bytes 2097152 | tf_op jit(solution)/shard_map/pallas_call | solution.py:231
  142.9 1.9 %reshape.317 = bf16[32,4,4,8,2,64]{5,4,3,2,1,0:T(2,128)(2,1)} reshape(bf16[16,2,4,32,128]{4,3,2,1,0:T(8,128)(2,1)S(1)} %shard_map.39) | data formatting | bytes 2097152 | tf_op jit(solution)/shard_map/reshape | solution.py:252
  144.8 0.1 cosine_multiply_fusion
  144.9 6.0 %fusion.2 = bf16[4,8,64,4,64]{2,4,1,0,3:T(8,128)(2,1)} fusion(bf16[32,4,4,8,2,64]{5,4,3,2,1,0:T(2,128)(2,1)} %reshape.317, f32[64,32,1]{0,1,2:T(8,128)S(1)} %get-tuple-element.10, f32[64,32,1]{0,1,2:T(8,128)S(1)} %get-tuple-element.9), kind=kOutput, calls=%fused_computation.3 | convolution fusion | flops 403705856 | bytes 2113536 | tf_op jit(solution)/shard_map/lfj,fgrcjd->rclgd/dot_general | solution.py:253
  150.9 3.1 %copy.8 = bf16[4,8,64,4,64]{4,3,2,1,0:T(4,128)(2,1)S(1)} copy(bf16[4,8,64,4,64]{2,4,1,0,3:T(8,128)(2,1)} %fusion.2) | data formatting | bytes 2097152 | tf_op jit(solution)/shard_map/convert_element_type | solution.py:254
  154.0 2.2 %reshape.318 = bf16[4,8,64,256]{3,2,1,0:T(8,128)(2,1)} reshape(bf16[4,8,64,4,64]{4,3,2,1,0:T(4,128)(2,1)S(1)} %copy.8) | data formatting | bytes 2097152 | tf_op jit(solution)/shard_map/reshape | solution.py:254
  (4 shorter events, 0.0 us)
Async XLA Ops:
  0.0 1.0 copy-start
  2.9 72.1 %copy-start.1 = (s32[4,16]{1,0:T(4,128)S(1)}, s32[4,16]{1,0:T(4,128)}, u32[]{:S(2)}) copy-start(s32[4,16]{1,0:T(4,128)} %partners.1) | copy-start | bytes 772

commit v2 on v0

v2 whole, which is shorter than its diff:
```python
from functools import partial
import math

import jax
import jax.numpy as jnp
from jax import lax
from jax.experimental import pallas as pl
from jax.experimental.pallas import tpu as pltpu
from jax.sharding import PartitionSpec as P

epsilon = 1e-06
MESH = pl.DeviceIdType.MESH
X, Y, Z, ZL, CORES = 4, 4, 16, 8, 2
ORDER = (1, 15, 2, 14, 3, 13, 4, 12, 5, 11, 6, 10, 7, 9, 8)
STEPS = (0, 1, 3, 2)


def forward_table(samples):
    sample_ids = jnp.arange(samples, dtype=jnp.int32)
    freq_ids = jnp.arange(1, samples // 2 + 1, dtype=jnp.int32)
    phases = (freq_ids[:, None] * sample_ids[None, :] % samples).astype(jnp.float32) * (
        2.0 * math.pi / samples
    )
    return jnp.stack([jnp.cos(phases), -jnp.sin(phases)], axis=1)


def lag_table(samples):
    shifts = jnp.arange(samples, dtype=jnp.int32) - samples // 2
    freq_ids = jnp.arange(1, samples // 2 + 1, dtype=jnp.int32)
    phases = (shifts[:, None] * freq_ids[None, :] % samples).astype(jnp.float32) * (
        2.0 * math.pi / samples
    )
    weights = jnp.where(freq_ids == samples // 2, 1.0, 2.0).astype(jnp.float32)[None, :]
    return jnp.stack([weights * jnp.cos(phases), weights * jnp.sin(phases)], axis=-1)


def whiten(raw, valid, samples):
    spectra = jnp.einsum(
        "fkt,wtc->wfkc",
        forward_table(samples),
        raw.astype(jnp.float32),
        precision=lax.Precision.HIGHEST,
    )
    band_power = jnp.mean(jnp.sum(spectra * spectra, axis=2), axis=-1)
    scaled = spectra * lax.rsqrt(band_power + epsilon)[:, :, None, None]
    return (scaled * valid.astype(jnp.float32)[:, None, None, None]).astype(jnp.bfloat16)


def place():
    pair, stack = lax.axis_index("pair"), lax.axis_index("stack")
    core = lax.rem(pair, 2)
    z_hi = lax.rem(lax.div(pair, 2), 2)
    return lax.div(pair, 4), lax.div(stack, ZL), z_hi * ZL + lax.rem(stack, ZL), core


def device(x, y, z, core):
    return (x * 4 + lax.div(z, ZL) * 2 + core, y * ZL + lax.rem(z, ZL))


def turn(index, by, size):
    return lax.rem(index + by, size)


def remote(src, dst, send, recv, to):
    return pltpu.make_async_remote_copy(
        src_ref=src, dst_ref=dst, send_sem=send, recv_sem=recv, device_id=to, device_id_type=MESH
    )


def local(src, dst, sem):
    return pltpu.make_async_copy(src, dst, sem)


def drain(ref, sem):
    pltpu.make_async_copy(ref, ref, sem).wait()


def exchange_kernel(partners, spec, out, landed, rows, cols_0, cols_1, parts, z_send, z_recv, xa_send, xa_recv,
                    ya_send, ya_recv, xg_send, xg_recv, yg_send, yg_recv, c_send, c_recv,
                    o_send, o_recv, here_z, here_x, here_y, here_o):
    x, y, z, core = place()
    cols = (cols_0, cols_1)
    z_hi, z_lo = lax.div(z, ZL), lax.rem(z, ZL)
    xs = [device(turn(x, d, X), y, z, core) for d in range(1, X)]
    ys = [device(x, turn(y, d, Y), z, core) for d in range(1, Y)]
    twin = device(x, y, z, 1 - core)

    def target(n):
        return (turn(x, lax.div(n, Z), X), turn(z_hi, lax.rem(lax.div(n, ZL), 2), 2),
                turn(z_lo, lax.rem(n, ZL), ZL))

    barrier = pltpu.get_barrier_semaphore()

    def greet(n, carry):
        tx, th, tl = target(n)
        pl.semaphore_signal(barrier, inc=1, device_id=device(tx, y, th * ZL + tl, core), device_id_type=MESH)
        return carry

    lax.fori_loop(1, 64, greet, 0)
    for peer in ys + [twin]:
        pl.semaphore_signal(barrier, inc=1, device_id=peer, device_id_type=MESH)
    pl.semaphore_wait(barrier, 67)

    quad = lax.div(z, 4)
    for chunk in range(2):
        local(spec.at[chunk, z], landed.at[chunk, z], here_z.at[chunk]).start()
        for by in ORDER:
            to = turn(z, by, Z)
            remote(spec.at[chunk, to], landed.at[chunk, z], z_send.at[chunk],
                   z_recv.at[chunk, quad], device(x, y, to, core)).start()

    def of_quad(q):
        return lax.div(q, 2), pl.ds(lax.rem(q, 2) * 4, 4)

    def to_groups(chunk, step):
        q = turn(quad, step, 4)
        hi, lo = of_quad(q)
        zs = pl.ds(q * 4, 4)
        if step == 0:
            drain(landed.at[chunk, pl.ds(0, 3)], z_recv.at[chunk, q])
            drain(landed.at[chunk, 0], here_z.at[chunk])
        else:
            drain(landed.at[chunk, zs], z_recv.at[chunk, q])
        for d in range(1, 4):
            tx, ty = turn(x, d, X), turn(y, d, Y)
            remote(landed.at[chunk, zs, tx], cols[chunk].at[x, hi, core, y, lo],
                   xa_send.at[chunk], xa_recv.at[chunk, step], xs[d - 1]).start()
            remote(landed.at[chunk, zs, ty], rows.at[chunk, x, hi, y, lo],
                   ya_send.at[chunk], ya_recv.at[chunk, step], ys[d - 1]).start()
        local(landed.at[chunk, zs, x], cols[chunk].at[x, hi, core, y, lo], here_x.at[chunk, step]).start()
        local(landed.at[chunk, zs, y], rows.at[chunk, x, hi, y, lo], here_y.at[chunk, step]).start()

    def to_planes(chunk, step):
        hi, lo = of_quad(turn(quad, step, 4))
        drain(cols[chunk].at[pl.ds(0, 3), hi, core, y, lo], xa_recv.at[chunk, step])
        drain(cols[chunk].at[0, hi, core, y, lo], here_x.at[chunk, step])
        for d in (1, 3, 2):
            part = cols[chunk].at[:, hi, core, y, lo]
            remote(part, part, yg_send.at[chunk], yg_recv.at[chunk, step], ys[d - 1]).start()
        drain(rows.at[chunk, x, hi, pl.ds(0, 3), lo], ya_recv.at[chunk, step])
        drain(rows.at[chunk, x, hi, 0, lo], here_y.at[chunk, step])
        for d in (1, 3, 2):
            part = rows.at[chunk, x, hi, :, lo]
            remote(part, part, xg_send.at[chunk], xg_recv.at[chunk, step], xs[d - 1]).start()

    def to_twin(chunk, step):
        hi, lo = of_quad(turn(quad, step, 4))
        drain(cols[chunk].at[:, hi, core, pl.ds(0, 3), lo], yg_recv.at[chunk, step])
        part = cols[chunk].at[:, hi, core, :, lo]
        remote(part, part, c_send.at[chunk], c_recv.at[chunk, step], twin).start()

    lanes = lax.broadcasted_iota(jnp.int32, (64, 128), 1)
    sign = jnp.where(lanes < 64, 1.0, -1.0).astype(jnp.float32)

    def whole(chunk, p):
        return cols[chunk][lax.div(p, 4), lax.rem(lax.div(p, 2), 2), lax.rem(p, 2)].reshape(512, 128)

    def cross(chunk):
        def block(n, carry):
            tx, th = turn(x, lax.div(n, 2), X), turn(z_hi, lax.rem(n, 2), 2)
            own = rows[chunk, tx, th].reshape(512, 128)
            p = tx * 4 + th * 2 + core
            picked = jnp.concatenate([whole(chunk, partners[r, p]) for r in range(4)], axis=1)
            both = lax.dot_general(own, picked, (((0,), (0,)), ((), ())),
                                   preferred_element_type=jnp.float32)
            found = []
            for r in range(4):
                at = both[:, 128 * r:128 * (r + 1)]
                part = at[:64] + sign * pltpu.roll(at[64:], 64, 1)
                found.append(part.reshape(8, 8, 128))
            first = pl.multiple_of((tx * 2 + th) * ZL, ZL)
            parts[chunk, pl.ds(first, ZL)] = jnp.concatenate(found, axis=1).astype(jnp.bfloat16)

            def send(low, carry):
                tl = turn(z_lo, low, ZL)
                remote(parts.at[chunk, first + tl], out.at[chunk, z * X + x], o_send.at[chunk],
                       o_recv.at[chunk], device(tx, y, th * ZL + tl, core)).start()
                return carry

            lax.fori_loop(jnp.where(n == 0, 1, 0), ZL, send, 0)
            return carry

        lax.fori_loop(0, 8, block, 0)
        local(parts.at[chunk, (x * 2 + z_hi) * ZL + z_lo], out.at[chunk, z * X + x], here_o.at[chunk]).start()

    for chunk in range(2):
        for at in range(len(STEPS) + 2):
            if at < 4:
                to_groups(chunk, STEPS[at])
            if 0 <= at - 1 < 4:
                to_planes(chunk, STEPS[at - 1])
            if 0 <= at - 2 < 4:
                to_twin(chunk, STEPS[at - 2])
        for step in STEPS:
            hi, lo = of_quad(turn(quad, step, 4))
            drain(rows.at[chunk, pl.ds(0, 3), hi, :, lo], xg_recv.at[chunk, step])
            drain(cols[chunk].at[:, hi, 1 - core, :, lo], c_recv.at[chunk, step])
        cross(chunk)

    for chunk in range(2):
        drain(out.at[chunk, pl.ds(0, 63)], o_recv.at[chunk])
        drain(out.at[chunk, 0], here_o.at[chunk])
        drain(spec.at[chunk, pl.ds(0, 15)], z_send.at[chunk])
        drain(landed.at[chunk, pl.ds(0, 12)], xa_send.at[chunk])
        drain(landed.at[chunk, pl.ds(0, 12)], ya_send.at[chunk])
        drain(rows.at[chunk, pl.ds(0, 3)], xg_send.at[chunk])
        drain(rows.at[chunk, pl.ds(0, 3)], yg_send.at[chunk])
        drain(rows.at[chunk], c_send.at[chunk])
        drain(parts.at[chunk, pl.ds(0, 63)], o_send.at[chunk])


def exchange(partners, spec):
    vmem = pl.BlockSpec(memory_space=pltpu.VMEM)
    dma = pltpu.SemaphoreType.DMA
    one, four = dma((2,)), dma((2, 4))
    return pl.pallas_call(
        exchange_kernel,
        out_shape=jax.ShapeDtypeStruct((2, Z * X, 32, 128), jnp.bfloat16),
        in_specs=[pl.BlockSpec(memory_space=pltpu.SMEM), vmem],
        out_specs=vmem,
        scratch_shapes=[
            pltpu.VMEM((2, Z, 4, 16, 128), jnp.bfloat16),
            pltpu.VMEM((2, X, 2, Y, ZL, 16, 128), jnp.bfloat16),
            pltpu.VMEM((X, 2, CORES, Y, ZL, 16, 128), jnp.bfloat16),
            pltpu.VMEM((X, 2, CORES, Y, ZL, 16, 128), jnp.bfloat16),
            pltpu.VMEM((2, 64, 32, 128), jnp.bfloat16),
        ] + [one, four] * 6 + [one, one, one, four, four, one],
        compiler_params=pltpu.CompilerParams(
            collective_id=0, has_side_effects=True, vmem_limit_bytes=40 << 20
        ),
        cost_estimate=pl.CostEstimate(flops=1 << 30, bytes_accessed=9 << 20, transcendentals=0),
    )(partners, spec)


def lag_kernel(got, table, out, spread):
    width = table.shape[-1]
    column = lax.rem(lax.broadcasted_iota(jnp.int32, (64, width), 1), 16)
    for row in range(16):
        keep = jnp.where(column == row, 1.0, 0.0).astype(jnp.bfloat16)
        for kind in range(4):
            spread[kind, pl.ds(64 * row, 64), :] = table[kind] * keep
    for half in range(2):
        real, imag = [], []
        for g in range(0, 4, 2):
            a = got[:, :, g, pl.ds(16 * half, 16), :].reshape(width, 128)
            b = got[:, :, g + 1, pl.ds(16 * half, 16), :].reshape(width, 128)
            real += [a[:, :64], b[:, :64]]
            imag += [a[:, 64:], b[:, 64:]]
        real, imag = jnp.concatenate(real, axis=1), jnp.concatenate(imag, axis=1)
        dot = partial(jnp.dot, preferred_element_type=jnp.float32)
        lagged = (dot(spread[0], real) + dot(spread[1], imag)) + (
            dot(spread[2], real) + dot(spread[3], imag))
        out[pl.ds(2 * half, 2)] = lagged.astype(jnp.bfloat16).reshape(2, 8, 64, 256)


def lag(got, windows):
    weights = lag_table(64) / windows
    weights = jnp.transpose(weights.reshape(64, Z, 2, 2), (3, 0, 2, 1)).reshape(2, 64, 32)
    high = weights.astype(jnp.bfloat16)
    low = (weights - high.astype(jnp.float32)).astype(jnp.bfloat16)
    table = jnp.repeat(jnp.concatenate([high, low]), 16, axis=2)
    vmem = pl.BlockSpec(memory_space=pltpu.VMEM)
    return pl.pallas_call(
        lag_kernel,
        out_shape=jax.ShapeDtypeStruct((4, 8, 64, 256), jnp.bfloat16),
        in_specs=[vmem, vmem],
        out_specs=vmem,
        scratch_shapes=[pltpu.VMEM((4, 1024, 512), jnp.bfloat16)],
        compiler_params=pltpu.CompilerParams(vmem_limit_bytes=40 << 20),
        cost_estimate=pl.CostEstimate(flops=1 << 31, bytes_accessed=3 << 20, transcendentals=0),
    )(got.reshape(2, Z, X, 32, 128), table)


def shards(raw, valid, partners):
    win_dev, samples, width = raw.shape
    whitened = whiten(raw, valid[:, 0], samples)
    spec = jnp.transpose(whitened.reshape(win_dev, Z, 2, 2, 4, 64), (2, 1, 4, 0, 3, 5))
    got = exchange(partners, spec.reshape(2, Z, 4, win_dev, 128))
    return lag(got, 512)


def solution(mesh):
    return jax.shard_map(
        shards,
        mesh=mesh,
        in_specs=(P("stack", None, "pair"), P("stack", "pair"), P()),
        out_specs=P(None, ("pair", "stack"), None, None),
        check_vma=False,
    )
```

time: 395 us -> 115 us (0.29)
  waiting for transfers between devices: 277 us -> 0 us
  Pallas kernels: 0 us -> 110 us
  blocking collectives: 45.2 us -> 0 us
  starting transfers between devices: 21.5 us -> 0 us
  matrix products: 21.4 us -> 0.63 us
  between operations: 13.7 us -> 0.12 us
  local copies, waits for them, and re-layouts: 12.2 us -> 2.42 us
    all_gather x1 -> x0, waiting for transfers between devices: 174 us -> none  [shards(): lax.all_gather(own_spec[:, :, None], 'pair', axis=2, tiled=True)]
    pallas_call x0 -> x2, Pallas kernels: none -> 110 us  [the longest x1 106 us: exchange(): pl.pallas_call(exchange_kernel, out_shape=jax.ShapeDtypeStruct((2, Z * X,...]
    all_to_all x4 -> x0, waiting for transfers between devices: 103 us -> none  [shards(): lax.all_to_all(jnp.stack([real_part, imag_part], axis=1), 'stack', split_...]
    all_to_all x1 -> x0, blocking collectives: 45.2 us -> none  [shards(): lax.all_to_all(whitened, 'stack', split_axis=1, concat_axis=0, tiled=True)]
    all_to_all x4 -> x0, starting transfers between devices: 21.4 us -> none  [shards(): lax.all_to_all(jnp.stack([real_part, imag_part], axis=1), 'stack', split_...]
    dot_general x14 -> x1, matrix products: 21.4 us -> 0.63 us  [whiten(): jnp.einsum('fkt,wtc->wfkc', forward_table(samples), raw.astype(jnp.float3...]
    slice x2 -> x0, local copies, waits for them, and re-layouts: 5.09 us -> none  [the longest x1 4.02 us: shards(): partner_now = partner_spec[:, :, pairing]]
    another operation x4 -> x0, local copies, waits for them, and re-layouts: 4.84 us -> none  [shards(): jnp.stack([real_part, imag_part], axis=1)]
  transfers between devices with their start and end apart: 5 -> 0, of which waited for: 5 -> 0; matrix products, arithmetic and copies ran while one was open for 4% -> 0% of each run, Pallas kernels for 0% -> 0%
where the time goes in v2:
time: 115 us; the launch traced here: 114 us
  Pallas kernels  110 us (96%)
  local copies, waits for them, and re-layouts  2.42 us (2%)
  other arithmetic  1.25 us (1%)
    pallas_call x1, Pallas kernels, exchange(): pl.pallas_call(exchange_kernel, out_shape=jax.ShapeDtypeStruct((2, Z * X,...  106 us
    pallas_call x1, Pallas kernels, lag(): pl.pallas_call(lag_kernel, out_shape=jax.ShapeDtypeStruct((4, 8, 64, 256)...  3.4 us

profile of v2, /device:TPU:1, one launch (start us, length us, event | category | flops | bytes accessed | tf_op | source)
XLA Modules:
  0.0 114.0 jit_solution(6059860482447800255)
XLA Ops:
  0.0 0.0 copy-start
  0.0 0.7 convert_bitcast_fusion
  0.7 0.1 cosine_multiply_fusion
  0.9 0.2 fusion.13
  1.1 0.1 broadcast_in_dim.20
  1.2 0.2 copy.6.table
  1.4 0.0 copy-done
  1.4 0.6 multiply_reduce_fusion
  2.0 0.2 multiply_convert_fusion
  2.2 0.4 reshape.281
  2.6 1.1 copy.9
  3.7 0.0 copy-start.1
  3.7 0.5 reshape.282.spec
  4.2 0.2 copy-done.1
  4.4 106.1 %shard_map.37 = bf16[2,64,32,128]{3,2,1,0:T(8,128)(2,1)S(1)} custom-call(s32[4,16]{1,0:T(4,128)S(1)} %copy-done.1, bf16[2,16,4,16,128]{4,3,2,1,0:T(8,128)(2,1)S(1)} %reshape.282.spec), custom_call_target="tpu_custom_call" | custom-call | flops 1073741824 | bytes 9437184 | tf_op jit(solution)/shard_map/pallas_call | solution.py:216
  110.6 3.4 %shard_map.38 = bf16[4,8,64,256]{3,2,1,0:T(8,128)(2,1)} custom-call(bf16[2,16,4,32,128]{4,3,2,1,0:T(8,128)(2,1)S(1)} %bitcast.33, bf16[4,64,512]{2,1,0:T(8,128)(2,1)S(1)} %copy.6.table), custom_call_target="tpu_custom_call" | custom-call | flops 2147483648 | bytes 3145728 | tf_op jit(solution)/shard_map/pallas_call | solution.py:263
  (8 shorter events, 0.1 us)
Async XLA Ops:
  0.0 1.4 %copy-start = (bf16[16,64,256]{2,1,0:T(8,128)(2,1)S(1)}, bf16[16,64,256]{2,1,0:T(8,128)(2,1)}, u32[]{:S(2)}) copy-start(bf16[16,64,256]{2,1,0:T(8,128)(2,1)} %param.3) | copy-start | bytes 1572868
  3.7 0.7 copy-start.1

commit v3 on v2

--- a/solution.py
+++ b/solution.py
@@ -3,6 +3,8 @@
 
 import jax
 import jax.numpy as jnp
+import ml_dtypes
+import numpy as np
 from jax import lax
 from jax.experimental import pallas as pl
 from jax.experimental.pallas import tpu as pltpu
@@ -13,37 +15,28 @@
 X, Y, Z, ZL, CORES = 4, 4, 16, 8, 2
 ORDER = (1, 15, 2, 14, 3, 13, 4, 12, 5, 11, 6, 10, 7, 9, 8)
 STEPS = (0, 1, 3, 2)
-
-
-def forward_table(samples):
-    sample_ids = jnp.arange(samples, dtype=jnp.int32)
-    freq_ids = jnp.arange(1, samples // 2 + 1, dtype=jnp.int32)
-    phases = (freq_ids[:, None] * sample_ids[None, :] % samples).astype(jnp.float32) * (
-        2.0 * math.pi / samples
-    )
-    return jnp.stack([jnp.cos(phases), -jnp.sin(phases)], axis=1)
-
-
-def lag_table(samples):
-    shifts = jnp.arange(samples, dtype=jnp.int32) - samples // 2
-    freq_ids = jnp.arange(1, samples // 2 + 1, dtype=jnp.int32)
-    phases = (shifts[:, None] * freq_ids[None, :] % samples).astype(jnp.float32) * (
-        2.0 * math.pi / samples
-    )
-    weights = jnp.where(freq_ids == samples // 2, 1.0, 2.0).astype(jnp.float32)[None, :]
-    return jnp.stack([weights * jnp.cos(phases), weights * jnp.sin(phases)], axis=-1)
-
-
-def whiten(raw, valid, samples):
-    spectra = jnp.einsum(
-        "fkt,wtc->wfkc",
-        forward_table(samples),
-        raw.astype(jnp.float32),
-        precision=lax.Precision.HIGHEST,
-    )
-    band_power = jnp.mean(jnp.sum(spectra * spectra, axis=2), axis=-1)
-    scaled = spectra * lax.rsqrt(band_power + epsilon)[:, :, None, None]
-    return (scaled * valid.astype(jnp.float32)[:, None, None, None]).astype(jnp.bfloat16)
+PLAN = [(stage, chunk, step) for chunk in (0, 1) for stage in "gpt" for step in range(4)]
+PLAN = PLAN[:12] + [("x", 0, 0)] + PLAN[12:] + [("x", 1, 0)]
+
+
+def split(table):
+    high = table.astype(ml_dtypes.bfloat16)
+    low = (table - high.astype(np.float64)).astype(ml_dtypes.bfloat16)
+    return np.stack([high, low])
+
+
+def forward_table():
+    freqs = 1 + 2 * np.arange(Z)[None, :, None] + np.arange(2)[:, None, None]
+    phases = freqs * np.arange(64) % 64 * (2.0 * math.pi / 64)
+    return split(np.stack([np.cos(phases), -np.sin(phases)])).reshape(128, 64)
+
+
+def lag_table(windows):
+    freqs = 1 + 2 * np.arange(Z)[None, :] + np.arange(2)[:, None]
+    phases = (np.arange(64) - 32)[:, None, None] * freqs % 64 * (2.0 * math.pi / 64)
+    weights = np.where(freqs == 32, 1.0, 2.0) / windows
+    table = split(np.stack([weights * np.cos(phases), weights * np.sin(phases)]))
+    return np.repeat(table.reshape(4, 64, 32), 16, axis=2)
 
 
 def place():
@@ -75,9 +68,25 @@
     pltpu.make_async_copy(ref, ref, sem).wait()
 
 
-def exchange_kernel(partners, spec, out, landed, rows, cols_0, cols_1, parts, z_send, z_recv, xa_send, xa_recv,
+def whiten(raw, valid, table, mixed, spec):
+    lanes = lax.broadcasted_iota(jnp.int32, (32, 128), 1)
+    for w in range(16):
+        both = jnp.dot(table[...], raw[w], preferred_element_type=jnp.float32)
+        spectra = both[:64] + both[64:]
+        re, im = spectra[:32], spectra[32:]
+        power = jnp.sum(re * re + im * im, axis=1, keepdims=True) * (1.0 / 256)
+        gain = lax.rsqrt(power + epsilon) * valid[w, 0].astype(jnp.float32)
+        re, im = re * gain, im * gain
+        for half in range(2):
+            a, b = re[:, 128 * half:128 * (half + 1)], im[:, 128 * half:128 * (half + 1)]
+            mixed[pl.ds(32 * half + w, 32, stride=64), :] = jnp.where(lanes < 64, a, pltpu.roll(b, 64, 1))
+            mixed[pl.ds(32 * half + 16 + w, 32, stride=64), :] = jnp.where(lanes < 64, pltpu.roll(a, 64, 1), b)
+    spec[...] = mixed[...].reshape(2, Z, 4, 16, 128).astype(jnp.bfloat16)
+
+
+def exchange_kernel(partners, valid, raw_hbm, table, out, raw, mixed, spec, landed, rows, cols_0, cols_1, parts, z_send, z_recv, xa_send, xa_recv,
                     ya_send, ya_recv, xg_send, xg_recv, yg_send, yg_recv, c_send, c_recv,
-                    o_send, o_recv, here_z, here_x, here_y, here_o):
+                    o_send, o_recv, here_z, here_x, here_y, here_o, fetched):
     x, y, z, core = place()
     cols = (cols_0, cols_1)
     z_hi, z_lo = lax.div(z, ZL), lax.rem(z, ZL)
@@ -85,20 +94,20 @@
     ys = [device(x, turn(y, d, Y), z, core) for d in range(1, Y)]
     twin = device(x, y, z, 1 - core)
 
-    def target(n):
-        return (turn(x, lax.div(n, Z), X), turn(z_hi, lax.rem(lax.div(n, ZL), 2), 2),
-                turn(z_lo, lax.rem(n, ZL), ZL))
-
+    fetch = local(raw_hbm, raw, fetched)
+    fetch.start()
     barrier = pltpu.get_barrier_semaphore()
 
     def greet(n, carry):
-        tx, th, tl = target(n)
-        pl.semaphore_signal(barrier, inc=1, device_id=device(tx, y, th * ZL + tl, core), device_id_type=MESH)
+        to = device(turn(x, lax.div(n, Z), X), y, turn(z, lax.rem(n, Z), Z), core)
+        pl.semaphore_signal(barrier, inc=1, device_id=to, device_id_type=MESH)
         return carry
 
     lax.fori_loop(1, 64, greet, 0)
     for peer in ys + [twin]:
         pl.semaphore_signal(barrier, inc=1, device_id=peer, device_id_type=MESH)
+    fetch.wait()
+    whiten(raw, valid, table, mixed, spec)
     pl.semaphore_wait(barrier, 67)
 
     quad = lax.div(z, 4)
@@ -155,47 +164,52 @@
     def whole(chunk, p):
         return cols[chunk][lax.div(p, 4), lax.rem(lax.div(p, 2), 2), lax.rem(p, 2)].reshape(512, 128)
 
+    def block(chunk, tx, th):
+        own = rows[chunk, tx, th].reshape(512, 128)
+        p = tx * 4 + th * 2 + core
+        picked = jnp.concatenate([whole(chunk, partners[r, p]) for r in range(4)], axis=1)
+        both = lax.dot_general(own, picked, (((0,), (0,)), ((), ())),
+                               preferred_element_type=jnp.float32)
+        found = []
+        for r in range(4):
+            at = both[:, 128 * r:128 * (r + 1)]
+            part = at[:64] + sign * pltpu.roll(at[64:], 64, 1)
+            found.append(part.reshape(8, 8, 128))
+        first = pl.multiple_of((tx * 2 + th) * ZL, ZL)
+        parts[chunk, pl.ds(first, ZL)] = jnp.concatenate(found, axis=1).astype(jnp.bfloat16)
+
     def cross(chunk):
-        def block(n, carry):
-            tx, th = turn(x, lax.div(n, 2), X), turn(z_hi, lax.rem(n, 2), 2)
-            own = rows[chunk, tx, th].reshape(512, 128)
-            p = tx * 4 + th * 2 + core
-            picked = jnp.concatenate([whole(chunk, partners[r, p]) for r in range(4)], axis=1)
-            both = lax.dot_general(own, picked, (((0,), (0,)), ((), ())),
-                                   preferred_element_type=jnp.float32)
-            found = []
-            for r in range(4):
-                at = both[:, 128 * r:128 * (r + 1)]
-                part = at[:64] + sign * pltpu.roll(at[64:], 64, 1)
-                found.append(part.reshape(8, 8, 128))
-            first = pl.multiple_of((tx * 2 + th) * ZL, ZL)
-            parts[chunk, pl.ds(first, ZL)] = jnp.concatenate(found, axis=1).astype(jnp.bfloat16)
-
-            def send(low, carry):
-                tl = turn(z_lo, low, ZL)
-                remote(parts.at[chunk, first + tl], out.at[chunk, z * X + x], o_send.at[chunk],
-                       o_recv.at[chunk], device(tx, y, th * ZL + tl, core)).start()
-                return carry
-
-            lax.fori_loop(jnp.where(n == 0, 1, 0), ZL, send, 0)
+        def blocks(d, carry):
+            tx = turn(x, d, X)
+            block(chunk, tx, 0)
+            block(chunk, tx, 1)
+
+            def send(by):
+                tz = turn(z, by, Z)
+                remote(parts.at[chunk, tx * Z + tz], out.at[chunk, z * X + x], o_send.at[chunk],
+                       o_recv.at[chunk], device(tx, y, tz, core)).start()
+
+            for by in ORDER:
+                send(by)
+            pl.when(d > 0)(lambda: send(0))
             return carry
 
-        lax.fori_loop(0, 8, block, 0)
-        local(parts.at[chunk, (x * 2 + z_hi) * ZL + z_lo], out.at[chunk, z * X + x], here_o.at[chunk]).start()
-
-    for chunk in range(2):
-        for at in range(len(STEPS) + 2):
-            if at < 4:
-                to_groups(chunk, STEPS[at])
-            if 0 <= at - 1 < 4:
-                to_planes(chunk, STEPS[at - 1])
-            if 0 <= at - 2 < 4:
-                to_twin(chunk, STEPS[at - 2])
+        lax.fori_loop(0, X, blocks, 0)
+        local(parts.at[chunk, x * Z + z], out.at[chunk, z * X + x], here_o.at[chunk]).start()
+
+    def ready(chunk):
         for step in STEPS:
             hi, lo = of_quad(turn(quad, step, 4))
             drain(rows.at[chunk, pl.ds(0, 3), hi, :, lo], xg_recv.at[chunk, step])
             drain(cols[chunk].at[:, hi, 1 - core, :, lo], c_recv.at[chunk, step])
-        cross(chunk)
+
+    work = {"g": to_groups, "p": to_planes, "t": to_twin}
+    for stage, chunk, step in PLAN:
+        if stage == "x":
+            ready(chunk)
+            cross(chunk)
+        else:
+            work[stage](chunk, STEPS[step])
 
     for chunk in range(2):
         drain(out.at[chunk, pl.ds(0, 63)], o_recv.at[chunk])
@@ -209,27 +223,30 @@
         drain(parts.at[chunk, pl.ds(0, 63)], o_send.at[chunk])
 
 
-def exchange(partners, spec):
-    vmem = pl.BlockSpec(memory_space=pltpu.VMEM)
+def exchange(raw, valid, partners):
+    vmem, smem = pl.BlockSpec(memory_space=pltpu.VMEM), pl.BlockSpec(memory_space=pltpu.SMEM)
     dma = pltpu.SemaphoreType.DMA
     one, four = dma((2,)), dma((2, 4))
     return pl.pallas_call(
         exchange_kernel,
         out_shape=jax.ShapeDtypeStruct((2, Z * X, 32, 128), jnp.bfloat16),
-        in_specs=[pl.BlockSpec(memory_space=pltpu.SMEM), vmem],
+        in_specs=[smem, smem, pl.BlockSpec(memory_space=pl.ANY), vmem],
         out_specs=vmem,
         scratch_shapes=[
+            pltpu.VMEM((16, 64, 256), jnp.bfloat16),
+            pltpu.VMEM((2048, 128), jnp.float32),
+            pltpu.VMEM((2, Z, 4, 16, 128), jnp.bfloat16),
             pltpu.VMEM((2, Z, 4, 16, 128), jnp.bfloat16),
             pltpu.VMEM((2, X, 2, Y, ZL, 16, 128), jnp.bfloat16),
             pltpu.VMEM((X, 2, CORES, Y, ZL, 16, 128), jnp.bfloat16),
             pltpu.VMEM((X, 2, CORES, Y, ZL, 16, 128), jnp.bfloat16),
             pltpu.VMEM((2, 64, 32, 128), jnp.bfloat16),
-        ] + [one, four] * 6 + [one, one, one, four, four, one],
+        ] + [one, four] * 6 + [one, one, one, four, four, one, dma],
         compiler_params=pltpu.CompilerParams(
             collective_id=0, has_side_effects=True, vmem_limit_bytes=40 << 20
         ),
         cost_estimate=pl.CostEstimate(flops=1 << 30, bytes_accessed=9 << 20, transcendentals=0),
-    )(partners, spec)
+    )(partners, valid, raw, jnp.asarray(forward_table()))
 
 
 def lag_kernel(got, table, out, spread):
@@ -254,11 +271,6 @@
 
 
 def lag(got, windows):
-    weights = lag_table(64) / windows
-    weights = jnp.transpose(weights.reshape(64, Z, 2, 2), (3, 0, 2, 1)).reshape(2, 64, 32)
-    high = weights.astype(jnp.bfloat16)
-    low = (weights - high.astype(jnp.float32)).astype(jnp.bfloat16)
-    table = jnp.repeat(jnp.concatenate([high, low]), 16, axis=2)
     vmem = pl.BlockSpec(memory_space=pltpu.VMEM)
     return pl.pallas_call(
         lag_kernel,
@@ -268,15 +280,11 @@
         scratch_shapes=[pltpu.VMEM((4, 1024, 512), jnp.bfloat16)],
         compiler_params=pltpu.CompilerParams(vmem_limit_bytes=40 << 20),
         cost_estimate=pl.CostEstimate(flops=1 << 31, bytes_accessed=3 << 20, transcendentals=0),
-    )(got.reshape(2, Z, X, 32, 128), table)
+    )(got.reshape(2, Z, X, 32, 128), jnp.asarray(lag_table(windows)))
 
 
 def shards(raw, valid, partners):
-    win_dev, samples, width = raw.shape
-    whitened = whiten(raw, valid[:, 0], samples)
-    spec = jnp.transpose(whitened.reshape(win_dev, Z, 2, 2, 4, 64), (2, 1, 4, 0, 3, 5))
-    got = exchange(partners, spec.reshape(2, Z, 4, win_dev, 128))
-    return lag(got, 512)
+    return lag(exchange(raw, valid, partners), 512)
 
 
 def solution(mesh):

time: 115 us -> 109 us (0.948)
  Pallas kernels: 110 us -> 106 us
  other arithmetic: 1.25 us -> 0 us
    pallas_call x1, Pallas kernels: 106 us -> 102 us  [exchange(): pl.pallas_call(exchange_kernel, out_shape=jax.ShapeDtypeStruct((2, Z * X,...]
    unnamed x4 -> x9, local copies, waits for them, and re-layouts: 0.19 us -> 2.55 us
    reshape x4 -> x0, local copies, waits for them, and re-layouts: 2.16 us -> none  [the longest x2 1.49 us: shards(): whitened.reshape(win_dev, Z, 2, 2, 4, 64)]
where the time goes in v3:
time: 109 us; the launch traced here: 108 us
  Pallas kernels  106 us (97%)
  local copies, waits for them, and re-layouts  2.55 us (2%)
    pallas_call x1, Pallas kernels, exchange(): pl.pallas_call(exchange_kernel, out_shape=jax.ShapeDtypeStruct((2, Z * X,...  102 us
    pallas_call x1, Pallas kernels, lag(): pl.pallas_call(lag_kernel, out_shape=jax.ShapeDtypeStruct((4, 8, 64, 256)...  3.4 us
    unnamed x9, local copies, waits for them, and re-layouts  2.55 us

profile of v3, /device:TPU:1, one launch (start us, length us, event | category | flops | bytes accessed | tf_op | source)
XLA Modules:
  0.0 108.3 jit_solution(14254628428613435166)
XLA Ops:
  0.0 0.0 copy-start.1
  0.0 0.7 copy.6.valid
  0.7 0.0 copy-done.1
  0.8 0.0 copy-start
  0.8 1.0 copy-done
  1.8 0.0 copy-start.3
  1.8 0.8 copy-done.3
  2.6 0.0 copy-start.2
  2.6 102.3 %shard_map.55 = bf16[2,64,32,128]{3,2,1,0:T(8,128)(2,1)S(1)} custom-call(s32[4,16]{1,0:T(4,128)S(1)} %copy-done.1, s32[16,1]{1,0:T(8,128)S(1)} %copy.6.valid, bf16[16,64,256]{2,1,0:T(8,128)(2,1)S(1)} %copy-done, bf16[128,64]{1,0:T(8,128)(2,1)S(1)} %copy-done.3), custom_call_target="tpu_custom_call" | custom-call | flops 1073741824 | bytes 9437184 | tf_op jit(solution)/shard_map/pallas_call | solution.py:230
  104.8 0.0 copy-done.2
  104.9 3.4 %shard_map.56 = bf16[4,8,64,256]{3,2,1,0:T(8,128)(2,1)} custom-call(bf16[2,16,4,32,128]{4,3,2,1,0:T(8,128)(2,1)S(1)} %bitcast.1, bf16[4,64,512]{2,1,0:T(8,128)(2,1)S(1)} %copy-done.2), custom_call_target="tpu_custom_call" | custom-call | flops 2147483648 | bytes 3145728 | tf_op jit(solution)/shard_map/pallas_call | solution.py:275
Async XLA Ops:
  0.0 0.7 copy-start.1
  0.8 1.0 copy-start
  1.8 0.8 copy-start.3
  2.6 102.3 %copy-start.2 = (bf16[4,64,512]{2,1,0:T(8,128)(2,1)S(1)}, bf16[4,64,512]{2,1,0:T(8,128)(2,1)}, u32[]{:S(2)}) copy-start(bf16[4,64,512]{2,1,0:T(8,128)(2,1)} %constant.5.clone.table) | copy-start | bytes 786436

commit v4 on v3

--- a/solution.py
+++ b/solution.py
@@ -68,14 +68,16 @@
     pltpu.make_async_copy(ref, ref, sem).wait()
 
 
-def whiten(raw, valid, table, mixed, spec):
+def whiten(raw, valid, tables, mixed, spec):
+    table = tables[4, :, :128].astype(jnp.bfloat16)
+    table = jnp.concatenate([table[:, :64], table[:, 64:]], axis=0)
     lanes = lax.broadcasted_iota(jnp.int32, (32, 128), 1)
     for w in range(16):
-        both = jnp.dot(table[...], raw[w], preferred_element_type=jnp.float32)
+        both = jnp.dot(table, raw[w], preferred_element_type=jnp.float32)
         spectra = both[:64] + both[64:]
         re, im = spectra[:32], spectra[32:]
         power = jnp.sum(re * re + im * im, axis=1, keepdims=True) * (1.0 / 256)
-        gain = lax.rsqrt(power + epsilon) * valid[w, 0].astype(jnp.float32)
+        gain = lax.rsqrt(power + epsilon) * valid[0, w].astype(jnp.float32)
         re, im = re * gain, im * gain
         for half in range(2):
             a, b = re[:, 128 * half:128 * (half + 1)], im[:, 128 * half:128 * (half + 1)]
@@ -84,31 +86,50 @@
     spec[...] = mixed[...].reshape(2, Z, 4, 16, 128).astype(jnp.bfloat16)
 
 
-def exchange_kernel(partners, valid, raw_hbm, table, out, raw, mixed, spec, landed, rows, cols_0, cols_1, parts, z_send, z_recv, xa_send, xa_recv,
-                    ya_send, ya_recv, xg_send, xg_recv, yg_send, yg_recv, c_send, c_recv,
-                    o_send, o_recv, here_z, here_x, here_y, here_o, fetched):
+def spread_table(tables, chunk, spread):
+    column = lax.rem(lax.broadcasted_iota(jnp.int32, (64, 256), 1), 16)
+    for row in range(16):
+        keep = jnp.where(column == row, 1.0, 0.0).astype(jnp.bfloat16)
+        for kind in range(4):
+            spread[kind, pl.ds(64 * row, 64), :] = tables[kind, :, 256 * chunk:256 * (chunk + 1)].astype(jnp.bfloat16) * keep
+
+
+def lag_sum(got, spread, half):
+    def rows(g):
+        groups = [got[z * X + g, pl.ds(16 * half, 16), :] for z in range(Z)]
+        return jnp.concatenate(groups, axis=0)
+
+    groups = [rows(g) for g in range(4)]
+    real = jnp.concatenate([g[:, :64] for g in groups], axis=1)
+    imag = jnp.concatenate([g[:, 64:] for g in groups], axis=1)
+    dot = partial(jnp.dot, preferred_element_type=jnp.float32)
+    return (dot(spread[0], real) + dot(spread[1], imag)) + (dot(spread[2], real) + dot(spread[3], imag))
+
+
+def kernel(partners_hbm, valid_hbm, raw_hbm, tables_hbm, out, partners, valid, tables,
+                    got_0, got_1, spread_0, spread_1, lagged, result, raw, mixed,
+                    spec, landed, rows, cols_0, cols_1, parts, z_send, z_recv, xa_send, xa_recv, ya_send,
+                    ya_recv, xg_send, xg_recv, yg_send, yg_recv, c_send, c_recv, o_send, o_recv, here_z,
+                    here_x, here_y, here_o, fetched, stored):
     x, y, z, core = place()
-    cols = (cols_0, cols_1)
+    cols, outs, spread = (cols_0, cols_1), (got_0, got_1), (spread_0, spread_1)
     z_hi, z_lo = lax.div(z, ZL), lax.rem(z, ZL)
     xs = [device(turn(x, d, X), y, z, core) for d in range(1, X)]
     ys = [device(x, turn(y, d, Y), z, core) for d in range(1, Y)]
     twin = device(x, y, z, 1 - core)
 
-    fetch = local(raw_hbm, raw, fetched)
-    fetch.start()
+    fetches = [local(*pair, fetched.at[n]) for n, pair in enumerate(
+        [(raw_hbm, raw), (tables_hbm, tables), (valid_hbm, valid), (partners_hbm, partners)])]
+    for fetch in fetches:
+        fetch.start()
     barrier = pltpu.get_barrier_semaphore()
-
-    def greet(n, carry):
-        to = device(turn(x, lax.div(n, Z), X), y, turn(z, lax.rem(n, Z), Z), core)
-        pl.semaphore_signal(barrier, inc=1, device_id=to, device_id_type=MESH)
-        return carry
-
-    lax.fori_loop(1, 64, greet, 0)
-    for peer in ys + [twin]:
+    peers = [device(x, y, turn(z, by, Z), core) for by in range(1, Z)] + xs + ys + [twin]
+    for peer in peers:
         pl.semaphore_signal(barrier, inc=1, device_id=peer, device_id_type=MESH)
-    fetch.wait()
-    whiten(raw, valid, table, mixed, spec)
-    pl.semaphore_wait(barrier, 67)
+    for fetch in fetches:
+        fetch.wait()
+    whiten(raw, valid, tables, mixed, spec)
+    pl.semaphore_wait(barrier, len(peers))
 
     quad = lax.div(z, 4)
     for chunk in range(2):
@@ -143,9 +164,10 @@
         hi, lo = of_quad(turn(quad, step, 4))
         drain(cols[chunk].at[pl.ds(0, 3), hi, core, y, lo], xa_recv.at[chunk, step])
         drain(cols[chunk].at[0, hi, core, y, lo], here_x.at[chunk, step])
+        part = cols[chunk].at[:, hi, core, y, lo]
         for d in (1, 3, 2):
-            part = cols[chunk].at[:, hi, core, y, lo]
-            remote(part, part, yg_send.at[chunk], yg_recv.at[chunk, step], ys[d - 1]).start()
+            remote(part, part, yg_send.at[chunk], yg_recv.at[chunk, step, d - 1], ys[d - 1]).start()
+        remote(part, part, c_send.at[chunk], c_recv.at[chunk, step], twin).start()
         drain(rows.at[chunk, x, hi, pl.ds(0, 3), lo], ya_recv.at[chunk, step])
         drain(rows.at[chunk, x, hi, 0, lo], here_y.at[chunk, step])
         for d in (1, 3, 2):
@@ -154,9 +176,10 @@
 
     def to_twin(chunk, step):
         hi, lo = of_quad(turn(quad, step, 4))
-        drain(cols[chunk].at[:, hi, core, pl.ds(0, 3), lo], yg_recv.at[chunk, step])
-        part = cols[chunk].at[:, hi, core, :, lo]
-        remote(part, part, c_send.at[chunk], c_recv.at[chunk, step], twin).start()
+        for d in (1, 3, 2):
+            part = cols[chunk].at[:, hi, core, turn(y, 4 - d, Y), lo]
+            drain(part, yg_recv.at[chunk, step, d - 1])
+            remote(part, part, c_send.at[chunk], c_recv.at[chunk, step], twin).start()
 
     lanes = lax.broadcasted_iota(jnp.int32, (64, 128), 1)
     sign = jnp.where(lanes < 64, 1.0, -1.0).astype(jnp.float32)
@@ -186,7 +209,7 @@
 
             def send(by):
                 tz = turn(z, by, Z)
-                remote(parts.at[chunk, tx * Z + tz], out.at[chunk, z * X + x], o_send.at[chunk],
+                remote(parts.at[chunk, tx * Z + tz], outs[chunk].at[z * X + x], o_send.at[chunk],
                        o_recv.at[chunk], device(tx, y, tz, core)).start()
 
             for by in ORDER:
@@ -195,7 +218,7 @@
             return carry
 
         lax.fori_loop(0, X, blocks, 0)
-        local(parts.at[chunk, x * Z + z], out.at[chunk, z * X + x], here_o.at[chunk]).start()
+        local(parts.at[chunk, x * Z + z], outs[chunk].at[z * X + x], here_o.at[chunk]).start()
 
     def ready(chunk):
         for step in STEPS:
@@ -212,8 +235,17 @@
             work[stage](chunk, STEPS[step])
 
     for chunk in range(2):
-        drain(out.at[chunk, pl.ds(0, 63)], o_recv.at[chunk])
-        drain(out.at[chunk, 0], here_o.at[chunk])
+        spread_table(tables, chunk, spread[chunk])
+    for chunk in range(2):
+        drain(outs[chunk].at[pl.ds(0, 63)], o_recv.at[chunk])
+        drain(outs[chunk].at[0], here_o.at[chunk])
+        for half in range(2):
+            if chunk == 0:
+                lagged[half] = lag_sum(got_0, spread_0, half)
+            else:
+                total = lagged[half] + lag_sum(got_1, spread_1, half)
+                result[pl.ds(2 * half, 2)] = total.astype(jnp.bfloat16).reshape(2, 8, 64, 256)
+                local(result.at[pl.ds(2 * half, 2)], out.at[pl.ds(2 * half, 2)], stored.at[half]).start()
         drain(spec.at[chunk, pl.ds(0, 15)], z_send.at[chunk])
         drain(landed.at[chunk, pl.ds(0, 12)], xa_send.at[chunk])
         drain(landed.at[chunk, pl.ds(0, 12)], ya_send.at[chunk])
@@ -221,18 +253,29 @@
         drain(rows.at[chunk, pl.ds(0, 3)], yg_send.at[chunk])
         drain(rows.at[chunk], c_send.at[chunk])
         drain(parts.at[chunk, pl.ds(0, 63)], o_send.at[chunk])
-
-
-def exchange(raw, valid, partners):
-    vmem, smem = pl.BlockSpec(memory_space=pltpu.VMEM), pl.BlockSpec(memory_space=pltpu.SMEM)
+    for half in range(2):
+        drain(result.at[pl.ds(2 * half, 2)], stored.at[half])
+
+
+def exchange(raw, valid, partners, tables):
+    hbm = pl.BlockSpec(memory_space=pltpu.HBM)
     dma = pltpu.SemaphoreType.DMA
     one, four = dma((2,)), dma((2, 4))
     return pl.pallas_call(
-        exchange_kernel,
-        out_shape=jax.ShapeDtypeStruct((2, Z * X, 32, 128), jnp.bfloat16),
-        in_specs=[smem, smem, pl.BlockSpec(memory_space=pl.ANY), vmem],
-        out_specs=vmem,
+        kernel,
+        out_shape=jax.ShapeDtypeStruct((4, 8, 64, 256), jnp.bfloat16),
+        in_specs=[hbm] * 4,
+        out_specs=hbm,
         scratch_shapes=[
+            pltpu.SMEM((4, 16), jnp.int32),
+            pltpu.SMEM((1, 16), jnp.int32),
+            pltpu.VMEM((5, 64, 512), jnp.float32),
+            pltpu.VMEM((Z * X, 32, 128), jnp.bfloat16),
+            pltpu.VMEM((Z * X, 32, 128), jnp.bfloat16),
+            pltpu.VMEM((4, 1024, 256), jnp.bfloat16),
+            pltpu.VMEM((4, 1024, 256), jnp.bfloat16),
+            pltpu.VMEM((2, 1024, 256), jnp.float32),
+            pltpu.VMEM((4, 8, 64, 256), jnp.bfloat16),
             pltpu.VMEM((16, 64, 256), jnp.bfloat16),
             pltpu.VMEM((2048, 128), jnp.float32),
             pltpu.VMEM((2, Z, 4, 16, 128), jnp.bfloat16),
@@ -241,50 +284,20 @@
             pltpu.VMEM((X, 2, CORES, Y, ZL, 16, 128), jnp.bfloat16),
             pltpu.VMEM((X, 2, CORES, Y, ZL, 16, 128), jnp.bfloat16),
             pltpu.VMEM((2, 64, 32, 128), jnp.bfloat16),
-        ] + [one, four] * 6 + [one, one, one, four, four, one, dma],
+        ] + [one, four] * 4 + [one, dma((2, 4, 3)), one, four] + [one, one, one, four, four, one, dma((4,)), one],
         compiler_params=pltpu.CompilerParams(
-            collective_id=0, has_side_effects=True, vmem_limit_bytes=40 << 20
+            collective_id=0, has_side_effects=True, vmem_limit_bytes=62 << 20
         ),
         cost_estimate=pl.CostEstimate(flops=1 << 30, bytes_accessed=9 << 20, transcendentals=0),
-    )(partners, valid, raw, jnp.asarray(forward_table()))
-
-
-def lag_kernel(got, table, out, spread):
-    width = table.shape[-1]
-    column = lax.rem(lax.broadcasted_iota(jnp.int32, (64, width), 1), 16)
-    for row in range(16):
-        keep = jnp.where(column == row, 1.0, 0.0).astype(jnp.bfloat16)
-        for kind in range(4):
-            spread[kind, pl.ds(64 * row, 64), :] = table[kind] * keep
-    for half in range(2):
-        real, imag = [], []
-        for g in range(0, 4, 2):
-            a = got[:, :, g, pl.ds(16 * half, 16), :].reshape(width, 128)
-            b = got[:, :, g + 1, pl.ds(16 * half, 16), :].reshape(width, 128)
-            real += [a[:, :64], b[:, :64]]
-            imag += [a[:, 64:], b[:, 64:]]
-        real, imag = jnp.concatenate(real, axis=1), jnp.concatenate(imag, axis=1)
-        dot = partial(jnp.dot, preferred_element_type=jnp.float32)
-        lagged = (dot(spread[0], real) + dot(spread[1], imag)) + (
-            dot(spread[2], real) + dot(spread[3], imag))
-        out[pl.ds(2 * half, 2)] = lagged.astype(jnp.bfloat16).reshape(2, 8, 64, 256)
-
-
-def lag(got, windows):
-    vmem = pl.BlockSpec(memory_space=pltpu.VMEM)
-    return pl.pallas_call(
-        lag_kernel,
-        out_shape=jax.ShapeDtypeStruct((4, 8, 64, 256), jnp.bfloat16),
-        in_specs=[vmem, vmem],
-        out_specs=vmem,
-        scratch_shapes=[pltpu.VMEM((4, 1024, 512), jnp.bfloat16)],
-        compiler_params=pltpu.CompilerParams(vmem_limit_bytes=40 << 20),
-        cost_estimate=pl.CostEstimate(flops=1 << 31, bytes_accessed=3 << 20, transcendentals=0),
-    )(got.reshape(2, Z, X, 32, 128), jnp.asarray(lag_table(windows)))
+    )(partners, valid.T, raw, tables)
 
 
 def shards(raw, valid, partners):
-    return lag(exchange(raw, valid, partners), 512)
+    tables = np.zeros((5, 64, 512), np.float32)
+    tables[:4] = lag_table(512)
+    tables[4, :, :128] = np.concatenate(np.split(forward_table(), 2), axis=1)
+    tables = jnp.asarray(tables)
+    return exchange(raw, valid, partners, tables)
 
 
 def solution(mesh):

time: 109 us -> 103 us (0.945)
  Pallas kernels: 106 us -> 101 us
    pallas_call x2 -> x1, Pallas kernels: 106 us -> 101 us  [exchange(): pl.pallas_call(kernel, out_shape=jax.ShapeDtypeStruct((4, 8, 64, 256), jn...]
    unnamed x9 -> x1, local copies, waits for them, and re-layouts: 2.55 us -> 2.3 us
where the time goes in v4:
time: 103 us
  Pallas kernels  101 us (98%)
  local copies, waits for them, and re-layouts  2.3 us (2%)
    pallas_call x1, Pallas kernels, exchange(): pl.pallas_call(kernel, out_shape=jax.ShapeDtypeStruct((4, 8, 64, 256), jn...  101 us
    unnamed x1, local copies, waits for them, and re-layouts  2.3 us

profile of v4, /device:TPU:1, one launch (start us, length us, event | category | flops | bytes accessed | tf_op | source)
XLA Modules:
  0.0 102.9 jit_solution(10643308738419872734)
XLA Ops:
  0.0 100.6 %shard_map.46 = bf16[4,8,64,256]{3,2,1,0:T(8,128)(2,1)} custom-call(s32[4,16]{1,0:T(4,128)} %partners_hbm.1, s32[1,16]{1,0:T(1,128)} %bitcast.1, bf16[16,64,256]{2,1,0:T(8,128)(2,1)} %raw_hbm.1, f32[5,64,512]{2,1,0:T(8,128)} %constant.2.clone.tables_hbm), custom_call_target="tpu_custom_call" | custom-call | flops 1073741824 | bytes 9437184 | tf_op jit(solution)/shard_map/pallas_call | solution.py:264
  100.6 2.3 %copy.6 = bf16[4,8,64,256]{3,2,1,0:T(8,128)(2,1)} copy(bf16[4,8,64,256]{3,2,1,0:T(8,128)(2,1)} %shard_map.46) | data formatting | bytes 2097152

commit v5 on v4

--- a/solution.py
+++ b/solution.py
@@ -14,9 +14,10 @@
 MESH = pl.DeviceIdType.MESH
 X, Y, Z, ZL, CORES = 4, 4, 16, 8, 2
 ORDER = (1, 15, 2, 14, 3, 13, 4, 12, 5, 11, 6, 10, 7, 9, 8)
-STEPS = (0, 1, 3, 2)
-PLAN = [(stage, chunk, step) for chunk in (0, 1) for stage in "gpt" for step in range(4)]
-PLAN = PLAN[:12] + [("x", 0, 0)] + PLAN[12:] + [("x", 1, 0)]
+PIECES = 4
+STEPS = {4: (0, 1, 3, 2), 2: (0, 1), 1: (0,)}[PIECES]
+DEPTH = Z // PIECES
+PLAN = [(stage, chunk) for chunk in (0, 1) for stage in "gptx"]
 
 
 def split(table):
@@ -131,23 +132,27 @@
     whiten(raw, valid, tables, mixed, spec)
     pl.semaphore_wait(barrier, len(peers))
 
-    quad = lax.div(z, 4)
+    piece = lax.div(z, DEPTH)
     for chunk in range(2):
         local(spec.at[chunk, z], landed.at[chunk, z], here_z.at[chunk]).start()
         for by in ORDER:
             to = turn(z, by, Z)
             remote(spec.at[chunk, to], landed.at[chunk, z], z_send.at[chunk],
-                   z_recv.at[chunk, quad], device(x, y, to, core)).start()
-
-    def of_quad(q):
-        return lax.div(q, 2), pl.ds(lax.rem(q, 2) * 4, 4)
+                   z_recv.at[chunk, piece], device(x, y, to, core)).start()
+
+    def part_of(q):
+        if PIECES == 1:
+            return slice(None), slice(None)
+        if PIECES == 2:
+            return q, slice(None)
+        return lax.div(q, 2), pl.ds(lax.rem(q, 2) * DEPTH, DEPTH)
 
     def to_groups(chunk, step):
-        q = turn(quad, step, 4)
-        hi, lo = of_quad(q)
-        zs = pl.ds(q * 4, 4)
+        q = turn(piece, step, PIECES)
+        hi, lo = part_of(q)
+        zs = pl.ds(q * DEPTH, DEPTH)
         if step == 0:
-            drain(landed.at[chunk, pl.ds(0, 3)], z_recv.at[chunk, q])
+            drain(landed.at[chunk, pl.ds(0, DEPTH - 1)], z_recv.at[chunk, q])
             drain(landed.at[chunk, 0], here_z.at[chunk])
         else:
             drain(landed.at[chunk, zs], z_recv.at[chunk, q])
@@ -161,7 +166,7 @@
         local(landed.at[chunk, zs, y], rows.at[chunk, x, hi, y, lo], here_y.at[chunk, step]).start()
 
     def to_planes(chunk, step):
-        hi, lo = of_quad(turn(quad, step, 4))
+        hi, lo = part_of(turn(piece, step, PIECES))
         drain(cols[chunk].at[pl.ds(0, 3), hi, core, y, lo], xa_recv.at[chunk, step])
         drain(cols[chunk].at[0, hi, core, y, lo], here_x.at[chunk, step])
         part = cols[chunk].at[:, hi, core, y, lo]
@@ -175,7 +180,7 @@
             remote(part, part, xg_send.at[chunk], xg_recv.at[chunk, step], xs[d - 1]).start()
 
     def to_twin(chunk, step):
-        hi, lo = of_quad(turn(quad, step, 4))
+        hi, lo = part_of(turn(piece, step, PIECES))
         for d in (1, 3, 2):
             part = cols[chunk].at[:, hi, core, turn(y, 4 - d, Y), lo]
             drain(part, yg_recv.at[chunk, step, d - 1])
@@ -202,8 +207,8 @@
         parts[chunk, pl.ds(first, ZL)] = jnp.concatenate(found, axis=1).astype(jnp.bfloat16)
 
     def cross(chunk):
-        def blocks(d, carry):
-            tx = turn(x, d, X)
+        def blocks(n, carry):
+            tx = turn(x, 3 - n, X)
             block(chunk, tx, 0)
             block(chunk, tx, 1)
 
@@ -212,9 +217,9 @@
                 remote(parts.at[chunk, tx * Z + tz], outs[chunk].at[z * X + x], o_send.at[chunk],
                        o_recv.at[chunk], device(tx, y, tz, core)).start()
 
-            for by in ORDER:
+            for by in ORDER[::-1]:
                 send(by)
-            pl.when(d > 0)(lambda: send(0))
+            pl.when(n < 3)(lambda: send(0))
             return carry
 
         lax.fori_loop(0, X, blocks, 0)
@@ -222,17 +227,18 @@
 
     def ready(chunk):
         for step in STEPS:
-            hi, lo = of_quad(turn(quad, step, 4))
+            hi, lo = part_of(turn(piece, step, PIECES))
             drain(rows.at[chunk, pl.ds(0, 3), hi, :, lo], xg_recv.at[chunk, step])
             drain(cols[chunk].at[:, hi, 1 - core, :, lo], c_recv.at[chunk, step])
 
     work = {"g": to_groups, "p": to_planes, "t": to_twin}
-    for stage, chunk, step in PLAN:
+    for stage, chunk in PLAN:
         if stage == "x":
             ready(chunk)
             cross(chunk)
         else:
-            work[stage](chunk, STEPS[step])
+            for step in STEPS:
+                work[stage](chunk, step)
 
     for chunk in range(2):
         spread_table(tables, chunk, spread[chunk])

time: 103 us -> 102 us (level)
  Pallas kernels: 101 us -> 99.7 us
where the time goes in v5:
time: 102 us
  Pallas kernels  99.7 us (98%)
  local copies, waits for them, and re-layouts  2.3 us (2%)
    pallas_call x1, Pallas kernels, exchange(): pl.pallas_call(kernel, out_shape=jax.ShapeDtypeStruct((4, 8, 64, 256), jn...  99.7 us
    unnamed x1, local copies, waits for them, and re-layouts  2.3 us

profile of v5, /device:TPU:1, one launch (start us, length us, event | category | flops | bytes accessed | tf_op | source)
XLA Modules:
  0.0 102.0 jit_solution(5063330864994726945)
XLA Ops:
  0.0 99.7 %shard_map.46 = bf16[4,8,64,256]{3,2,1,0:T(8,128)(2,1)} custom-call(s32[4,16]{1,0:T(4,128)} %partners_hbm.1, s32[1,16]{1,0:T(1,128)} %bitcast.1, bf16[16,64,256]{2,1,0:T(8,128)(2,1)} %raw_hbm.1, f32[5,64,512]{2,1,0:T(8,128)} %constant.2.clone.tables_hbm), custom_call_target="tpu_custom_call" | custom-call | flops 1073741824 | bytes 9437184 | tf_op jit(solution)/shard_map/pallas_call | solution.py:270
  99.7 2.3 %copy.6 = bf16[4,8,64,256]{3,2,1,0:T(8,128)(2,1)} copy(bf16[4,8,64,256]{3,2,1,0:T(8,128)(2,1)} %shard_map.46) | data formatting | bytes 2097152

commit v6 on v5

--- a/solution.py
+++ b/solution.py
@@ -124,7 +124,7 @@
     for fetch in fetches:
         fetch.start()
     barrier = pltpu.get_barrier_semaphore()
-    peers = [device(x, y, turn(z, by, Z), core) for by in range(1, Z)] + xs + ys + [twin]
+    peers = [device(x, y, turn(z, by, Z), core) for by in ORDER[::-1]] + xs + ys + [twin]
     for peer in peers:
         pl.semaphore_signal(barrier, inc=1, device_id=peer, device_id_type=MESH)
     for fetch in fetches:
@@ -298,12 +298,37 @@
     )(partners, valid.T, raw, tables)
 
 
+def copy_kernel(src, out, held, sems):
+    takes = [local(src.at[r], held.at[r], sems.at[r]) for r in range(4)]
+    gives = [local(held.at[r], out.at[r], sems.at[r + 4]) for r in range(4)]
+    for take in takes:
+        take.start()
+    for take, give in zip(takes, gives):
+        take.wait()
+        give.start()
+    for give in gives:
+        give.wait()
+
+
+def hand_over(lagged):
+    hbm = pl.BlockSpec(memory_space=pltpu.HBM)
+    return pl.pallas_call(
+        copy_kernel,
+        out_shape=jax.ShapeDtypeStruct((4, 8, 64, 256), jnp.bfloat16),
+        in_specs=[hbm],
+        out_specs=hbm,
+        scratch_shapes=[pltpu.VMEM((4, 8, 64, 256), jnp.bfloat16), pltpu.SemaphoreType.DMA((8,))],
+        compiler_params=pltpu.CompilerParams(vmem_limit_bytes=62 << 20),
+        cost_estimate=pl.CostEstimate(flops=0, bytes_accessed=2 << 20, transcendentals=0),
+    )(lagged)
+
+
 def shards(raw, valid, partners):
     tables = np.zeros((5, 64, 512), np.float32)
     tables[:4] = lag_table(512)
     tables[4, :, :128] = np.concatenate(np.split(forward_table(), 2), axis=1)
     tables = jnp.asarray(tables)
-    return exchange(raw, valid, partners, tables)
+    return hand_over(exchange(raw, valid, partners, tables))
 
 
 def solution(mesh):

time: 102 us -> 102 us (level)
  local copies, waits for them, and re-layouts: 2.3 us -> 0 us
  Pallas kernels: 99.7 us -> 102 us
    unnamed x1 -> x0, local copies, waits for them, and re-layouts: 2.3 us -> none
    pallas_call x0 -> x1, Pallas kernels: none -> 1.98 us  [hand_over(): pl.pallas_call(copy_kernel, out_shape=jax.ShapeDtypeStruct((4, 8, 64, 256...]
where the time goes in v6:
time: 102 us
  Pallas kernels  102 us (100%)
    pallas_call x1, Pallas kernels, exchange(): pl.pallas_call(kernel, out_shape=jax.ShapeDtypeStruct((4, 8, 64, 256), jn...  99.7 us

profile of v6, /device:TPU:1, one launch (start us, length us, event | category | flops | bytes accessed | tf_op | source)
XLA Modules:
  0.0 101.7 jit_solution(13685410797983406077)
XLA Ops:
  0.0 99.7 %shard_map.46.src = bf16[4,8,64,256]{3,2,1,0:T(8,128)(2,1)} custom-call(s32[4,16]{1,0:T(4,128)} %partners_hbm.1, s32[1,16]{1,0:T(1,128)} %bitcast.1, bf16[16,64,256]{2,1,0:T(8,128)(2,1)} %raw_hbm.1, f32[5,64,512]{2,1,0:T(8,128)} %constant.2.clone.tables_hbm), custom_call_target="tpu_custom_call" | custom-call | flops 1073741824 | bytes 9437184 | tf_op jit(solution)/shard_map/pallas_call | solution.py:270
  99.7 2.0 %shard_map.47 = bf16[4,8,64,256]{3,2,1,0:T(8,128)(2,1)} custom-call(bf16[4,8,64,256]{3,2,1,0:T(8,128)(2,1)} %shard_map.46.src), custom_call_target="tpu_custom_call" | custom-call | bytes 2097152 | tf_op jit(solution)/shard_map/pallas_call | solution.py:315

commit v7 on v6

--- a/solution.py
+++ b/solution.py
@@ -17,7 +17,7 @@
 PIECES = 4
 STEPS = {4: (0, 1, 3, 2), 2: (0, 1), 1: (0,)}[PIECES]
 DEPTH = Z // PIECES
-PLAN = [(stage, chunk) for chunk in (0, 1) for stage in "gptx"]
+PLAN = [(stage, chunk) for chunk in (0, 1) for stage in "gpotx"]
 
 
 def split(table):
@@ -110,7 +110,8 @@
 def kernel(partners_hbm, valid_hbm, raw_hbm, tables_hbm, out, partners, valid, tables,
                     got_0, got_1, spread_0, spread_1, lagged, result, raw, mixed,
                     spec, landed, rows, cols_0, cols_1, parts, z_send, z_recv, xa_send, xa_recv, ya_send,
-                    ya_recv, xg_send, xg_recv, yg_send, yg_recv, c_send, c_recv, o_send, o_recv, here_z,
+                    ya_recv, xg_send, xg_recv, yg_send, yg_recv, xf_send,
+                    xf_recv, yf_send, yf_recv, c_send, c_recv, o_send, o_recv, here_z,
                     here_x, here_y, here_o, fetched, stored):
     x, y, z, core = place()
     cols, outs, spread = (cols_0, cols_1), (got_0, got_1), (spread_0, spread_1)
@@ -133,12 +134,15 @@
     pl.semaphore_wait(barrier, len(peers))
 
     piece = lax.div(z, DEPTH)
-    for chunk in range(2):
+
+    def to_plane(chunk):
         local(spec.at[chunk, z], landed.at[chunk, z], here_z.at[chunk]).start()
         for by in ORDER:
             to = turn(z, by, Z)
             remote(spec.at[chunk, to], landed.at[chunk, z], z_send.at[chunk],
                    z_recv.at[chunk, piece], device(x, y, to, core)).start()
+
+    to_plane(0)
 
     def part_of(q):
         if PIECES == 1:
@@ -170,20 +174,38 @@
         drain(cols[chunk].at[pl.ds(0, 3), hi, core, y, lo], xa_recv.at[chunk, step])
         drain(cols[chunk].at[0, hi, core, y, lo], here_x.at[chunk, step])
         part = cols[chunk].at[:, hi, core, y, lo]
-        for d in (1, 3, 2):
-            remote(part, part, yg_send.at[chunk], yg_recv.at[chunk, step, d - 1], ys[d - 1]).start()
+        for side in range(2):
+            remote(part, part, yg_send.at[chunk], yg_recv.at[chunk, step, side], ys[2 * side]).start()
         remote(part, part, c_send.at[chunk], c_recv.at[chunk, step], twin).start()
         drain(rows.at[chunk, x, hi, pl.ds(0, 3), lo], ya_recv.at[chunk, step])
         drain(rows.at[chunk, x, hi, 0, lo], here_y.at[chunk, step])
-        for d in (1, 3, 2):
-            part = rows.at[chunk, x, hi, :, lo]
-            remote(part, part, xg_send.at[chunk], xg_recv.at[chunk, step], xs[d - 1]).start()
+        part = rows.at[chunk, x, hi, :, lo]
+        for side in range(2):
+            remote(part, part, xg_send.at[chunk], xg_recv.at[chunk, step, side], xs[2 * side]).start()
+
+    def onward(chunk, step):
+        hi, lo = part_of(turn(piece, step, PIECES))
+        for side in range(2):
+            came = turn(y, 3 - 2 * side, Y)
+            part = cols[chunk].at[:, hi, core, came, lo]
+            drain(part, yg_recv.at[chunk, step, side])
+            part = cols[chunk].at[pl.ds(2 * side, 2), hi, core, came, lo]
+            remote(part, part, yf_send.at[chunk], yf_recv.at[chunk, step, side], ys[2 * side]).start()
+        for side in range(2):
+            came = turn(x, 3 - 2 * side, X)
+            part = rows.at[chunk, came, hi, :, lo]
+            drain(part, xg_recv.at[chunk, step, side])
+            part = rows.at[chunk, came, hi, pl.ds(2 * side, 2), lo]
+            remote(part, part, xf_send.at[chunk], xf_recv.at[chunk, step, side], xs[2 * side]).start()
+        for side in range(2):
+            part = cols[chunk].at[:, hi, core, turn(y, 3 - 2 * side, Y), lo]
+            remote(part, part, c_send.at[chunk], c_recv.at[chunk, step], twin).start()
 
     def to_twin(chunk, step):
         hi, lo = part_of(turn(piece, step, PIECES))
-        for d in (1, 3, 2):
-            part = cols[chunk].at[:, hi, core, turn(y, 4 - d, Y), lo]
-            drain(part, yg_recv.at[chunk, step, d - 1])
+        for side in range(2):
+            part = cols[chunk].at[pl.ds(2 * side, 2), hi, core, turn(y, 2, Y), lo]
+            drain(part, yf_recv.at[chunk, step, side])
             remote(part, part, c_send.at[chunk], c_recv.at[chunk, step], twin).start()
 
     lanes = lax.broadcasted_iota(jnp.int32, (64, 128), 1)
@@ -228,10 +250,11 @@
     def ready(chunk):
         for step in STEPS:
             hi, lo = part_of(turn(piece, step, PIECES))
-            drain(rows.at[chunk, pl.ds(0, 3), hi, :, lo], xg_recv.at[chunk, step])
+            for side in range(2):
+                drain(rows.at[chunk, turn(x, 2, X), hi, pl.ds(2 * side, 2), lo], xf_recv.at[chunk, step, side])
             drain(cols[chunk].at[:, hi, 1 - core, :, lo], c_recv.at[chunk, step])
 
-    work = {"g": to_groups, "p": to_planes, "t": to_twin}
+    work = {"g": to_groups, "p": to_planes, "o": onward, "t": to_twin}
     for stage, chunk in PLAN:
         if stage == "x":
             ready(chunk)
@@ -239,6 +262,8 @@
         else:
             for step in STEPS:
                 work[stage](chunk, step)
+        if (stage, chunk) == ("g", 0):
+            to_plane(1)
 
     for chunk in range(2):
         spread_table(tables, chunk, spread[chunk])
@@ -255,8 +280,10 @@
         drain(spec.at[chunk, pl.ds(0, 15)], z_send.at[chunk])
         drain(landed.at[chunk, pl.ds(0, 12)], xa_send.at[chunk])
         drain(landed.at[chunk, pl.ds(0, 12)], ya_send.at[chunk])
-        drain(rows.at[chunk, pl.ds(0, 3)], xg_send.at[chunk])
-        drain(rows.at[chunk, pl.ds(0, 3)], yg_send.at[chunk])
+        for sent in (xg_send, yg_send):
+            drain(rows.at[chunk, pl.ds(0, 2)], sent.at[chunk])
+        for sent in (xf_send, yf_send):
+            drain(rows.at[chunk, 0], sent.at[chunk])
         drain(rows.at[chunk], c_send.at[chunk])
         drain(parts.at[chunk, pl.ds(0, 63)], o_send.at[chunk])
     for half in range(2):
@@ -266,7 +293,7 @@
 def exchange(raw, valid, partners, tables):
     hbm = pl.BlockSpec(memory_space=pltpu.HBM)
     dma = pltpu.SemaphoreType.DMA
-    one, four = dma((2,)), dma((2, 4))
+    one, four = dma((2,)), dma((2, PIECES))
     return pl.pallas_call(
         kernel,
         out_shape=jax.ShapeDtypeStruct((4, 8, 64, 256), jnp.bfloat16),
@@ -290,7 +317,7 @@
             pltpu.VMEM((X, 2, CORES, Y, ZL, 16, 128), jnp.bfloat16),
             pltpu.VMEM((X, 2, CORES, Y, ZL, 16, 128), jnp.bfloat16),
             pltpu.VMEM((2, 64, 32, 128), jnp.bfloat16),
-        ] + [one, four] * 4 + [one, dma((2, 4, 3)), one, four] + [one, one, one, four, four, one, dma((4,)), one],
+        ] + [one, four] * 3 + [one, dma((2, PIECES, 2))] * 4 + [one, four] + [one, one, one, four, four, one, dma((4,)), one],
         compiler_params=pltpu.CompilerParams(
             collective_id=0, has_side_effects=True, vmem_limit_bytes=62 << 20
         ),

time: 102 us -> 99 us (0.971)
  Pallas kernels: 102 us -> 98.8 us
    pallas_call x1, Pallas kernels: 99.7 us -> 96.8 us  [exchange(): pl.pallas_call(kernel, out_shape=jax.ShapeDtypeStruct((4, 8, 64, 256), jn...]
where the time goes in v7:
time: 99 us; the launch traced here: 98.8 us
  Pallas kernels  98.8 us (100%)
    pallas_call x1, Pallas kernels, exchange(): pl.pallas_call(kernel, out_shape=jax.ShapeDtypeStruct((4, 8, 64, 256), jn...  96.8 us
    pallas_call x1, Pallas kernels, hand_over(): pl.pallas_call(copy_kernel, out_shape=jax.ShapeDtypeStruct((4, 8, 64, 256...  1.98 us

profile of v7, /device:TPU:1, one launch (start us, length us, event | category | flops | bytes accessed | tf_op | source)
XLA Modules:
  0.0 98.8 jit_solution(10610114759971016229)
XLA Ops:
  0.0 96.8 %shard_map.46.src = bf16[4,8,64,256]{3,2,1,0:T(8,128)(2,1)} custom-call(s32[4,16]{1,0:T(4,128)} %partners_hbm.1, s32[1,16]{1,0:T(1,128)} %bitcast.1, bf16[16,64,256]{2,1,0:T(8,128)(2,1)} %raw_hbm.1, f32[5,64,512]{2,1,0:T(8,128)} %constant.2.clone.tables_hbm), custom_call_target="tpu_custom_call" | custom-call | flops 1073741824 | bytes 9437184 | tf_op jit(solution)/shard_map/pallas_call | solution.py:297
  96.9 2.0 %shard_map.47 = bf16[4,8,64,256]{3,2,1,0:T(8,128)(2,1)} custom-call(bf16[4,8,64,256]{3,2,1,0:T(8,128)(2,1)} %shard_map.46.src), custom_call_target="tpu_custom_call" | custom-call | bytes 2097152 | tf_op jit(solution)/shard_map/pallas_call | solution.py:342
